TPU v7x, 256 devices: a whole 4x4x8 slice. The times are simulated.
256 devices in a mesh: group: 8 (over x, core), inner: 32 (over z, y).
Axes of the slice: x: 4, y: 4, z: 8, core: 2. Of those that a mesh axis runs over, the one named last changes fastest.
Arguments:
- features: bfloat16 [524288, 256], P(('group', 'inner')), may hold values from -6 to 6
- w_self: bfloat16 [256, 256], replicated, may hold values from -0.375 to 0.375
- w_neigh: bfloat16 [256, 256], replicated, may hold values from -0.375 to 0.375
- node_bias: float32 [256], replicated, may hold values from -3 to 3
- grad_out: bfloat16 [524288, 256], P(('group', 'inner')), may hold values from -6 to 6
- send_rows: int32 [256, 32, 8, 8], P(('group', 'inner')), may hold values from 0 to 2047
- send_count: int32 [256, 32, 8], P(('group', 'inner')), may hold values from 0 to 8, as said below
- adjacency: int32 [256, 16, 2, 128, 128], P(('group', 'inner')), may hold values from 0 to 2
- tile_source: int32 [256, 16, 2], P(('group', 'inner')), may hold values from 0 to 31, as said below
Outputs:
- output: bfloat16 [524288, 256], P(('group', 'inner'))
- grad_features: bfloat16 [524288, 256], P(('group', 'inner'))
- grad_self: float32 [256, 256], replicated
- grad_neigh: float32 [256, 256], replicated
- grad_bias: float32 [256], replicated
Inputs may be any that keep to these rules, and one draw needn't show every extreme that they name: `send_count`: A device's block to itself is empty; each device fills all 8 slots of its block to the next device of its own group; the other blocks within a group hold at least half of the slots. `tile_source`: the first tile of each destination block reads a block of the device's own rows, the others read blocks of halo rows.
All inputs are finite; a program needn't handle non-finite values.
Results may differ from a plain program's by a relative error of at most 0.0075.
Values may be sent and summed in bfloat16 or wider, within the bound.
A program may use at most 64 MiB of HBM per device.

v0:
```python
import math

import jax
import jax.numpy as jnp
from jax import lax
from jax.sharding import PartitionSpec as P


def contract_rows(left, right):
    return lax.dot_general(
        left, right, (((0,), (0,)), ((), ())), preferred_element_type=jnp.float32
    )


def contract_cols(left, right):
    return lax.dot_general(
        left, right, (((1,), (1,)), ((), ())), preferred_element_type=jnp.float32
    )


def local(
    features, w_self, w_neigh, node_bias, grad_out, send_rows, send_count, adjacency, tile_source
):
    node_count, width = features.shape
    slot_rows = send_rows[0]
    inner_count, group_count, slots = slot_rows.shape
    keep_slot = lax.broadcasted_iota(jnp.int32, slot_rows.shape, 2) < send_count[0][:, :, None]
    gathered = features[slot_rows.reshape(-1)].reshape(inner_count, group_count, slots, width)
    outgoing = jnp.where(keep_slot[..., None], gathered, jnp.zeros((), jnp.bfloat16))
    sectioned = lax.all_to_all(outgoing, "group", split_axis=1, concat_axis=1, tiled=True)
    halo_rows = lax.all_to_all(sectioned, "inner", split_axis=0, concat_axis=0, tiled=True)
    extended = jnp.concatenate([features, halo_rows.reshape(-1, width)], axis=0)
    tile_edge = adjacency.shape[-1]
    blocks = extended.reshape(-1, tile_edge, width)
    sources = tile_source[0]
    picked = blocks[sources]
    adj_tiles = adjacency[0]
    adj_values = adj_tiles.astype(jnp.bfloat16)
    summed = jnp.einsum("dkrc,dkch->drh", adj_values, picked, preferred_element_type=jnp.float32)
    degree = jnp.sum(adj_tiles, axis=(1, 3))
    inverse = 1.0 / jnp.maximum(degree, 1).astype(jnp.float32)
    mean_agg = (summed * inverse[..., None]).reshape(node_count, width).astype(jnp.bfloat16)
    pre_act = jnp.dot(features, w_self, preferred_element_type=jnp.float32)
    pre_act = pre_act + jnp.dot(mean_agg, w_neigh, preferred_element_type=jnp.float32) + node_bias
    sigma = jax.nn.sigmoid(pre_act)
    output = (pre_act * sigma).astype(jnp.bfloat16)
    slope = sigma * (1.0 + pre_act * (1.0 - sigma))
    grad_pre = (grad_out.astype(jnp.float32) * slope).astype(jnp.bfloat16)
    part_self = contract_rows(features, grad_pre)
    part_neigh = contract_rows(mean_agg, grad_pre)
    part_bias = jnp.sum(grad_pre.astype(jnp.float32), axis=0)
    summed_grads = lax.psum((part_self, part_neigh, part_bias), ("group", "inner"))
    factor = 1.0 / math.sqrt(node_count * lax.axis_size("group") * lax.axis_size("inner"))
    back_self = contract_cols(grad_pre, w_self)
    back_agg = contract_cols(grad_pre, w_neigh).reshape(-1, tile_edge, width)
    back_agg = (back_agg * inverse[..., None]).astype(jnp.bfloat16)
    picked_grad = jnp.einsum(
        "dkrc,drh->dkch", adj_values, back_agg, preferred_element_type=jnp.float32
    )
    ext_grad = jnp.zeros(blocks.shape, jnp.float32)
    ext_grad = ext_grad.at[sources.reshape(-1)].add(picked_grad.reshape(-1, tile_edge, width))
    ext_grad = ext_grad.reshape(-1, width)
    halo_grad = (
        ext_grad[node_count:].reshape(inner_count, group_count, slots, width).astype(jnp.bfloat16)
    )
    partway = lax.all_to_all(halo_grad, "inner", split_axis=0, concat_axis=0, tiled=True)
    returned = lax.all_to_all(partway, "group", split_axis=1, concat_axis=1, tiled=True)
    masked = jnp.where(
        keep_slot[..., None], returned.astype(jnp.float32), jnp.zeros((), jnp.float32)
    )
    grad_total = back_self + ext_grad[:node_count]
    grad_total = grad_total.at[slot_rows.reshape(-1)].add(masked.reshape(-1, width))
    return (
        output,
        grad_total.astype(jnp.bfloat16),
        summed_grads[0] * factor,
        summed_grads[1] * factor,
        summed_grads[2] * factor,
    )


def solution(mesh):
    placed = (
        P(("group", "inner"), None),
        P(),
        P(),
        P(),
        P(("group", "inner"), None),
        P(("group", "inner"), None, None, None),
        P(("group", "inner"), None, None),
        P(("group", "inner"), None, None, None, None),
        P(("group", "inner"), None, None),
    )
    return jax.shard_map(
        local,
        mesh=mesh,
        in_specs=placed,
        out_specs=(P(("group", "inner"), None), P(("group", "inner"), None), P(), P(), P()),
        check_vma=False,
    )
```

profile of v0, /device:TPU:1, one launch (start us, length us, event | category | flops | bytes accessed | tf_op | source)
XLA Modules:
  0.0 440.9 jit_solution(9971950850001759671)
XLA Ops:
  7.2 0.0 copy-start
  7.2 0.8 iota_compare_fusion
  8.0 0.9 copy.54
  8.9 0.1 reshape_squeeze.7
  9.0 8.0 %gather_fusion = bf16[2048,256]{1,0:T(8,128)(2,1)S(1)} fusion(bf16[2048,256]{1,0:T(8,128)(2,1)} %param.9, s32[2048]{0:T(1024)S(1)} %broadcast_clamp_fusion), kind=kCustom, calls=%fused_computation | custom fusion | bytes 2105344 | tf_op jit(solution)/shard_map/gather | solution.py:28
  17.0 0.4 copy_select_fusion
  17.5 20.7 %all_to_all.20 = bf16[32,8,8,256]{3,2,0,1:T(8,128)(2,1)S(1)} all-to-all(bf16[32,8,8,256]{3,2,0,1:T(8,128)(2,1)S(1)} %copy_select_fusion), channel_id=1, replica_groups=mesh['group'=8,'inner'=32] {'group'}, dimensions={1} | all-to-all | bytes 2097152 | tf_op jit(solution)/shard_map/all_to_all | solution.py:30
  38.2 1.1 copy.56
  39.3 11.4 %all-to-all-start.1 = ((bf16[32,8,8,256]{3,2,1,0:T(8,128)(2,1)}), bf16[32,8,8,256]{3,2,1,0:T(8,128)(2,1)}, u32[]{:S(2)}, u32[]{:S(2)}) async-start(bf16[32,8,8,256]{3,2,1,0:T(8,128)(2,1)} %copy.56), calls=%async_computation.1 | async-start | bytes 2097152 | tf_op jit(solution)/shard_map/all_to_all | solution.py:31
  50.7 0.1 copy.58
  50.8 0.1 copy.57
  50.9 0.1 reshape.148
  51.0 0.1 reshape_squeeze.8
  51.1 0.3 reduce_sum.18
  51.5 1.8 fusion.11
  53.3 23.2 %all-to-all-done.1 = bf16[32,8,8,256]{3,2,1,0:T(8,128)(2,1)} async-done(((bf16[32,8,8,256]{3,2,1,0:T(8,128)(2,1)}), bf16[32,8,8,256]{3,2,1,0:T(8,128)(2,1)}, u32[]{:S(2)}, u32[]{:S(2)}) %all-to-all-start.1) | async-done | bytes 1048608 | tf_op jit(solution)/shard_map/all_to_all | solution.py:31
  76.5 2.7 pad_maximum_fusion
  79.2 3.6 gather_fusion.1
  82.8 2.2 fusion.1
  85.1 0.2 copy-done.9
  85.3 2.2 convert_reduce_fusion
  87.5 1.0 copy-done.3
  88.5 1.8 fusion.12
  90.3 2.9 copy.59
  93.2 4.3 fusion.3
  97.5 5.6 %copy.60 = f32[32,128,256]{2,1,0:T(8,128)} copy(f32[32,128,256]{1,2,0:T(8,128)} %bitcast.54) | data formatting | bytes 8388608 | tf_op jit(solution)/shard_map/reshape | solution.py:61
  103.1 2.5 broadcast_in_dim.36
  105.5 10.0 %scatter_fusion = f32[32,128,256]{2,1,0:T(8,128)} fusion(f32[32,128,256]{2,1,0:T(8,128)} %broadcast_in_dim.36, s32[32]{0:T(128)S(1)} %fusion.10, f32[32,128,256]{2,1,0:T(8,128)} %copy.60), kind=kCustom, calls=%fused_computation.2 | custom fusion | flops 1048576 | bytes 12583040 | tf_op jit(solution)/shard_map/scatter-add | solution.py:61
  115.5 2.8 slice.21
  118.3 6.5 %all-to-all-start.2 = ((bf16[32,8,8,256]{3,2,1,0:T(8,128)(2,1)}), bf16[32,8,8,256]{3,2,1,0:T(8,128)(2,1)S(1)}, u32[]{:S(2)}, u32[]{:S(2)}) async-start(bf16[32,8,8,256]{3,2,1,0:T(8,128)(2,1)} %bitcast.60), calls=%async_computation.2 | async-start | bytes 2097152 | tf_op jit(solution)/shard_map/all_to_all | solution.py:66
  124.8 2.5 fusion.13
  127.2 22.5 %all-to-all-done.2 = bf16[32,8,8,256]{3,2,1,0:T(8,128)(2,1)S(1)} async-done(((bf16[32,8,8,256]{3,2,1,0:T(8,128)(2,1)}), bf16[32,8,8,256]{3,2,1,0:T(8,128)(2,1)S(1)}, u32[]{:S(2)}, u32[]{:S(2)}) %all-to-all-start.2) | async-done | bytes 1048608 | tf_op jit(solution)/shard_map/all_to_all | solution.py:66
  149.8 1.0 copy.61
  150.8 8.1 %all-to-all-start.3 = ((bf16[32,8,8,256]{3,2,0,1:T(8,128)(2,1)}), bf16[32,8,8,256]{3,2,0,1:T(8,128)(2,1)}, u32[]{:S(2)}, u32[]{:S(2)}) async-start(bf16[32,8,8,256]{3,2,0,1:T(8,128)(2,1)} %copy.61), calls=%async_computation.3 | async-start | bytes 2097152 | tf_op jit(solution)/shard_map/all_to_all | solution.py:67
  158.9 1.2 convolution_bitcast_fusion
  160.1 3.1 slice.18
  163.2 0.0 all-reduce.3.cloned.1.call-update
  163.2 2.1 convolution_add_fusion
  165.3 76.6 %psum.23 = f32[256]{0:T(256)S(1)} all-reduce(f32[256]{0:T(256)S(1)} %get-tuple-element.32), channel_id=1, replica_groups=mesh['group'=8,'inner'=32] {'group','inner'}, use_global_device_ids=true, to_apply=%region_6.7 | all-reduce | flops 256 | bytes 2048 | tf_op jit(solution)/shard_map/psum | solution.py:52
  241.9 0.6 broadcast_multiply_fusion.2
  242.4 171.7 %all-reduce.3.cloned.1.call-done = (f32[256,256]{0,1:T(8,128)}, f32[256,256]{0,1:T(8,128)}) async-done(((f32[256,256]{0,1:T(8,128)}, f32[256,256]{0,1:T(8,128)}), (f32[256,256]{0,1:T(8,128)}, f32[256,256]{0,1:T(8,128)})) %all-reduce.3.cloned.1.call-update) | async-done | bytes 524304 | tf_op jit(solution)/shard_map/psum | solution.py:52
  414.2 1.1 broadcast_multiply_fusion
  415.3 0.8 copy.65
  416.1 0.8 copy.64
  416.9 1.6 convert_select_fusion
  418.5 1.6 copy.62
  420.1 12.9 %scatter_fusion.1 = f32[2048,256]{1,0:T(8,128)S(1)} fusion(f32[2048,256]{1,0:T(8,128)S(1)} %convolution_add_fusion, s32[2048]{0:T(1024)S(1)} %bitcast.65, f32[2048,256]{1,0:T(8,128)} %bitcast.55), kind=kCustom, calls=%fused_computation.3 | custom fusion | flops 524288 | bytes 6299648 | tf_op jit(solution)/shard_map/scatter-add | solution.py:72
  433.0 1.1 convert_element_type.59
  (27 shorter events, 0.1 us)
Async XLA Ops:
  7.2 77.9 %copy-start = (bf16[256,256]{1,0:T(8,128)(2,1)S(1)}, bf16[256,256]{1,0:T(8,128)(2,1)}, u32[]{:S(2)}) copy-start(bf16[256,256]{1,0:T(8,128)(2,1)} %param.11) | copy-start | bytes 393220
  38.2 12.5 %copy-start.8 = (s32[1,16,2]{1,2,0:T(2,128)S(1)}, s32[1,16,2]{1,2,0:T(2,128)}, u32[]{:S(2)}) copy-start(s32[1,16,2]{1,2,0:T(2,128)} %param.17) | copy-start | bytes 388
  38.2 12.9 %copy-start.2 = (s32[1,16,2,128,128]{4,3,2,1,0:T(8,128)S(1)}, s32[1,16,2,128,128]{4,3,2,1,0:T(8,128)}, u32[]{:S(2)}) copy-start(s32[1,16,2,128,128]{4,3,2,1,0:T(8,128)} %param.16) | copy-start | bytes 6291460
  39.3 12.2 %copy-start.1 = (bf16[2048,256]{1,0:T(8,128)(2,1)S(1)}, bf16[2048,256]{1,0:T(8,128)(2,1)}, u32[]{:S(2)}) copy-start(bf16[2048,256]{1,0:T(8,128)(2,1)} %param.9) | copy-start | bytes 3145732
  39.3 12.2 %copy-start.7 = (bf16[256,256]{1,0:T(8,128)(2,1)S(1)}, bf16[256,256]{1,0:T(8,128)(2,1)}, u32[]{:S(2)}) copy-start(bf16[256,256]{1,0:T(8,128)(2,1)} %param.10) | copy-start | bytes 393220
  39.3 37.2 %all-to-all-start.1 = ((bf16[32,8,8,256]{3,2,1,0:T(8,128)(2,1)}), bf16[32,8,8,256]{3,2,1,0:T(8,128)(2,1)}, u32[]{:S(2)}, u32[]{:S(2)}) async-start(bf16[32,8,8,256]{3,2,1,0:T(8,128)(2,1)} %copy.56), calls=%async_computation.1 | async-start | bytes 2097152 | tf_op jit(solution)/shard_map/all_to_all | solution.py:31
  82.8 2.3 copy-start.5
  82.8 2.5 copy-start.9
  82.8 2.5 copy-start.10
  85.1 2.4 copy-start.6
  87.5 1.0 copy-start.3
  115.5 9.3 %copy-start.4 = (bf16[2048,256]{1,0:T(8,128)(2,1)S(1)}, bf16[2048,256]{1,0:T(8,128)(2,1)}, u32[]{:S(2)}) copy-start(bf16[2048,256]{1,0:T(8,128)(2,1)} %copy-done.3) | copy-start | bytes 3145732
  118.3 31.5 %all-to-all-start.2 = ((bf16[32,8,8,256]{3,2,1,0:T(8,128)(2,1)}), bf16[32,8,8,256]{3,2,1,0:T(8,128)(2,1)S(1)}, u32[]{:S(2)}, u32[]{:S(2)}) async-start(bf16[32,8,8,256]{3,2,1,0:T(8,128)(2,1)} %bitcast.60), calls=%async_computation.2 | async-start | bytes 2097152 | tf_op jit(solution)/shard_map/all_to_all | solution.py:66
  150.8 266.1 %all-to-all-start.3 = ((bf16[32,8,8,256]{3,2,0,1:T(8,128)(2,1)}), bf16[32,8,8,256]{3,2,0,1:T(8,128)(2,1)}, u32[]{:S(2)}, u32[]{:S(2)}) async-start(bf16[32,8,8,256]{3,2,0,1:T(8,128)(2,1)} %copy.61), calls=%async_computation.3 | async-start | bytes 2097152 | tf_op jit(solution)/shard_map/all_to_all | solution.py:67
  158.9 255.3 %all-reduce.3.cloned.1.call-start = ((), (), s32[]{:S(2)}) async-start(), calls=%async_computation.4 | async-start | bytes 1048576 | tf_op jit(solution)/shard_map/psum | solution.py:52
Sparse Core Ops, SparseCore 0:
  165.9 248.2 all-reduce.2
where the time goes:
time: 443 us; the launch traced here: 441 us
  waiting for transfers between devices  218 us (49%)
  blocking collectives  97.3 us (22%)
  local copies, waits for them, and re-layouts  36.4 us (8%)
  other arithmetic  31.5 us (7%)
  starting transfers between devices  26 us (6%)
  matrix products  18 us (4%)
  between operations  14.2 us (3%)
    psum x1, waiting for transfers between devices, local(): lax.psum((part_self, part_neigh, part_bias), ('group', 'inner'))  172 us
    psum x1, blocking collectives, local(): lax.psum((part_self, part_neigh, part_bias), ('group', 'inner'))  76.6 us
    all_to_all x1, waiting for transfers between devices, local(): lax.all_to_all(sectioned, 'inner', split_axis=0, concat_axis=0, tiled=True)  23.2 us
    all_to_all x1, waiting for transfers between devices, local(): lax.all_to_all(halo_grad, 'inner', split_axis=0, concat_axis=0, tiled=True)  22.5 us
    all_to_all x1, blocking collectives, local(): lax.all_to_all(outgoing, 'group', split_axis=1, concat_axis=1, tiled=True)  20.7 us
    scatter-add x1, other arithmetic, local(): grad_total.at[slot_rows.reshape(-1)].add(masked.reshape(-1, width))  12.9 us
    all_to_all x1, starting transfers between devices, local(): lax.all_to_all(sectioned, 'inner', split_axis=0, concat_axis=0, tiled=True)  11.4 us
    scatter-add x1, other arithmetic, local(): ext_grad.at[sources.reshape(-1)]  9.96 us
  transfers between devices with their start and end apart: 4, of which 3 were waited for; matrix products, arithmetic and copies ran while one was open for 3% of the time, Pallas kernels for 0%

commit v1 on v0

--- a/solution.py
+++ b/solution.py
@@ -3,7 +3,11 @@
 import jax
 import jax.numpy as jnp
 from jax import lax
+from jax.experimental import pallas as pl
+from jax.experimental.pallas import tpu as pltpu
 from jax.sharding import PartitionSpec as P
+
+MESH = pl.DeviceIdType.MESH
 
 
 def contract_rows(left, right):
@@ -18,6 +22,55 @@
     )
 
 
+def exchange_kernel(x, y, ssem, rsem, lsem):
+    g, j = lax.axis_index("group"), lax.axis_index("inner")
+    z, yy, cx, cc = j // 4, j % 4, g // 2, g % 2
+    me = j * 8 + g
+    own = pltpu.make_async_copy(x.at[me], y.at[me], lsem)
+    own.start()
+    barrier = pltpu.get_barrier_semaphore()
+
+    def greet(t, carry):
+        d = lax.rem(me + t, 256)
+        pl.semaphore_signal(barrier, inc=1, device_id=(d % 8, d // 8), device_id_type=MESH)
+        return carry
+
+    lax.fori_loop(1, 256, greet, 0)
+    pl.semaphore_wait(barrier, 255)
+    for k in range(8):
+        dz = (4, 3, 5, 2, 6, 1, 7, 0)[k]
+
+        def send(m, carry):
+            h = ((cx + m // 8) % 4) * 2 + (cc + m // 4) % 2
+            i = ((z + dz) % 8) * 4 + (yy + m) % 4
+            pltpu.make_async_remote_copy(
+                x.at[i * 8 + h], y.at[me], ssem.at[k], rsem.at[k], device_id=(h, i), device_id_type=MESH
+            ).start()
+            return carry
+
+        lax.fori_loop(1 if dz == 0 else 0, 32, send, 0)
+    for k in range(8):
+        n = 31 if k == 7 else 32
+        part = pltpu.make_async_remote_copy(
+            x.at[pl.ds(0, n)], y.at[pl.ds(0, n)], ssem.at[k], rsem.at[k], device_id=(g, j), device_id_type=MESH
+        )
+        part.wait()
+    own.wait()
+
+
+def exchange(x, cid):
+    inner, group, slots, width = x.shape
+    t = x.reshape(inner * group, slots, 2, width // 2).transpose(0, 2, 1, 3).reshape(inner * group, 2 * slots, width // 2)
+    y = pl.pallas_call(
+        exchange_kernel,
+        out_shape=jax.ShapeDtypeStruct(t.shape, t.dtype),
+        in_specs=[pl.BlockSpec(memory_space=pltpu.VMEM)],
+        out_specs=pl.BlockSpec(memory_space=pltpu.VMEM),
+        scratch_shapes=[pltpu.SemaphoreType.DMA((8,)), pltpu.SemaphoreType.DMA((8,)), pltpu.SemaphoreType.DMA],
+        compiler_params=pltpu.CompilerParams(collective_id=0, has_side_effects=True, vmem_limit_bytes=16 << 20),
+    )(t)
+    return y.reshape(inner, group, 2, slots, width // 2).transpose(0, 1, 3, 2, 4).reshape(x.shape)
+
 def local(
     features, w_self, w_neigh, node_bias, grad_out, send_rows, send_count, adjacency, tile_source
 ):
@@ -27,8 +80,7 @@
     keep_slot = lax.broadcasted_iota(jnp.int32, slot_rows.shape, 2) < send_count[0][:, :, None]
     gathered = features[slot_rows.reshape(-1)].reshape(inner_count, group_count, slots, width)
     outgoing = jnp.where(keep_slot[..., None], gathered, jnp.zeros((), jnp.bfloat16))
-    sectioned = lax.all_to_all(outgoing, "group", split_axis=1, concat_axis=1, tiled=True)
-    halo_rows = lax.all_to_all(sectioned, "inner", split_axis=0, concat_axis=0, tiled=True)
+    halo_rows = exchange(outgoing, 0)
     extended = jnp.concatenate([features, halo_rows.reshape(-1, width)], axis=0)
     tile_edge = adjacency.shape[-1]
     blocks = extended.reshape(-1, tile_edge, width)
@@ -63,8 +115,7 @@
     halo_grad = (
         ext_grad[node_count:].reshape(inner_count, group_count, slots, width).astype(jnp.bfloat16)
     )
-    partway = lax.all_to_all(halo_grad, "inner", split_axis=0, concat_axis=0, tiled=True)
-    returned = lax.all_to_all(partway, "group", split_axis=1, concat_axis=1, tiled=True)
+    returned = exchange(halo_grad, 1)
     masked = jnp.where(
         keep_slot[..., None], returned.astype(jnp.float32), jnp.zeros((), jnp.float32)
     )

time: 443 us -> 346 us (0.78)
  waiting for transfers between devices: 218 us -> 93.5 us
  Pallas kernels: 0 us -> 80.4 us
  starting transfers between devices: 26 us -> 0.04 us
  blocking collectives: 97.3 us -> 74.5 us
  local copies, waits for them, and re-layouts: 36.4 us -> 31.2 us
    pallas_call x0 -> x2, Pallas kernels: none -> 80.4 us  [exchange(): pl.pallas_call(exchange_kernel, out_shape=jax.ShapeDtypeStruct(t.shape, t...]
    psum x1, waiting for transfers between devices: 172 us -> 93.5 us  [local(): lax.psum((part_self, part_neigh, part_bias), ('group', 'inner'))]
    all_to_all x3 -> x0, waiting for transfers between devices: 45.8 us -> none  [the longest x1 23.2 us: local(): lax.all_to_all(sectioned, 'inner', split_axis=0, concat_axis=0, tiled=True)]
    all_to_all x3 -> x0, starting transfers between devices: 26 us -> none  [the longest x1 11.4 us: local(): lax.all_to_all(sectioned, 'inner', split_axis=0, concat_axis=0, tiled=True)]
    all_to_all x1 -> x0, blocking collectives: 20.7 us -> none  [local(): lax.all_to_all(outgoing, 'group', split_axis=1, concat_axis=1, tiled=True)]
  transfers between devices with their start and end apart: 4 -> 1, of which waited for: 3 -> 1; matrix products, arithmetic and copies ran while one was open for 3% -> 15% of each run, Pallas kernels for 0% -> 11%
where the time goes in v1:
time: 346 us; the launch traced here: 344 us
  waiting for transfers between devices  93.5 us (27%)
  Pallas kernels  80.4 us (23%)
  blocking collectives  74.5 us (22%)
  other arithmetic  32.7 us (9%)
  local copies, waits for them, and re-layouts  31.2 us (9%)
  matrix products  17.7 us (5%)
  between operations  14.2 us (4%)
    psum x1, waiting for transfers between devices, local(): lax.psum((part_self, part_neigh, part_bias), ('group', 'inner'))  93.5 us
    pallas_call x2, Pallas kernels, exchange(): pl.pallas_call(exchange_kernel, out_shape=jax.ShapeDtypeStruct(t.shape, t...  80.4 us
    psum x1, blocking collectives, local(): lax.psum((part_self, part_neigh, part_bias), ('group', 'inner'))  74.5 us
    scatter-add x1, other arithmetic, local(): grad_total.at[slot_rows.reshape(-1)].add(masked.reshape(-1, width))  15.6 us
    scatter-add x1, other arithmetic, local(): ext_grad.at[sources.reshape(-1)]  10.1 us
    gather x1, local copies, waits for them, and re-layouts, local(): features[slot_rows.reshape(-1)]  8 us
  transfers between devices with their start and end apart: 1, of which 1 were waited for; matrix products, arithmetic and copies ran while one was open for 15% of the time, Pallas kernels for 11%

profile of v1, /device:TPU:1, one launch (start us, length us, event | category | flops | bytes accessed | tf_op | source)
XLA Modules:
  0.0 344.2 jit_solution(12410977075196604524)
XLA Ops:
  7.2 0.0 copy-start
  7.2 0.0 all-reduce.3.cloned.1.call-start
  7.2 0.9 copy.23
  8.1 0.1 reshape_squeeze.7
  8.3 0.8 copy.22
  9.0 0.1 lt.61
  9.1 0.1 iota_compare_fusion.1
  9.2 8.0 %gather_fusion = bf16[2048,256]{1,0:T(8,128)(2,1)S(1)} fusion(bf16[2048,256]{1,0:T(8,128)(2,1)} %param.9, s32[2048]{0:T(1024)S(1)} %broadcast_clamp_fusion), kind=kCustom, calls=%fused_computation | custom fusion | bytes 2105344 | tf_op jit(solution)/shard_map/gather | solution.py:81
  17.3 0.4 fusion.9.x
  17.7 42.9 %shard_map.128 = bf16[256,16,128]{2,1,0:T(8,128)(2,1)S(1)} custom-call(bf16[256,16,128]{2,1,0:T(8,128)(2,1)S(1)} %fusion.9.x), custom_call_target="tpu_custom_call" | custom-call | tf_op jit(solution)/shard_map/pallas_call | solution.py:64
  60.7 1.4 pad_maximum_fusion
  62.1 0.1 copy.24
  62.2 0.1 reshape.175
  62.3 0.7 copy-done.2
  63.0 0.3 reduce_sum.18
  63.4 1.8 fusion.16
  65.2 3.6 %gather_fusion.1 = bf16[32,128,256]{2,1,0:T(8,128)(2,1)} fusion(bf16[32,128,256]{2,1,0:T(8,128)(2,1)} %bitcast.78, s32[1024]{0:T(1024)S(1)} %pad_clamp_fusion), kind=kCustom, calls=%fused_computation.1 | custom fusion | bytes 4194432 | tf_op jit(solution)/shard_map/gather | solution.py:88
  68.8 2.2 fusion.1
  71.0 0.2 copy-done.9
  71.2 2.2 convert_reduce_fusion
  73.5 1.2 fusion.18
  74.7 1.2 convolution_bitcast_fusion
  75.9 0.0 all-reduce.3.cloned.1.call-update
  75.9 3.0 fusion.17
  78.9 0.1 copy.25
  79.0 2.9 copy.26
  81.9 4.3 %fusion.5 = f32[16,256,2,128]{3,1,2,0:T(8,128)} fusion(f32[16,128,256]{1,2,0:T(8,128)} %copy.26, f32[16,128]{1,0:T(8,128)S(1)} %convert_divide_fusion, s32[1,16,2,128,128]{4,3,2,1,0:T(8,128)S(1)} %copy-done.2), kind=kOutput, calls=%fused_computation.20 | convolution fusion | flops 270008320 | bytes 8396800 | tf_op jit(solution)/shard_map/dkrc,drh->dkch/dot_general | solution.py:109
  86.2 5.6 %copy.27 = f32[32,128,256]{2,1,0:T(8,128)} copy(f32[32,128,256]{1,2,0:T(8,128)} %bitcast.76) | data formatting | bytes 8388608 | tf_op jit(solution)/shard_map/reshape | solution.py:113
  91.8 0.1 reshape_squeeze.8
  91.9 2.5 broadcast_in_dim.38
  94.3 10.1 %scatter_fusion = f32[32,128,256]{2,1,0:T(8,128)} fusion(f32[32,128,256]{2,1,0:T(8,128)} %broadcast_in_dim.38, s32[32]{0:T(128)S(1)} %fusion.15, f32[32,128,256]{2,1,0:T(8,128)} %copy.27), kind=kCustom, calls=%fused_computation.2 | custom fusion | flops 1048576 | bytes 12583040 | tf_op jit(solution)/shard_map/scatter-add | solution.py:113
  104.4 1.8 slice.18
  106.2 0.0 copy-done.4
  106.3 1.8 convolution_add_fusion
  108.1 0.1 copy.28
  108.2 0.1 iota_compare_fusion
  108.3 1.7 slice.21
  110.0 37.5 %shard_map.129 = bf16[256,16,128]{2,1,0:T(8,128)(2,1)S(1)} custom-call(bf16[256,16,128]{2,1,0:T(8,128)(2,1)S(1)} %bitcast.74), custom_call_target="tpu_custom_call" | custom-call | tf_op jit(solution)/shard_map/pallas_call | solution.py:64
  147.5 0.2 convert.7
  147.7 0.1 lt.72
  147.9 15.6 %scatter_custom_fusion.1 = f32[2048,256]{1,0:T(8,128)} fusion(f32[2048,256]{1,0:T(8,128)} %convolution_add_fusion, s32[2048]{0:T(1024)S(1)} %bitcast.85, f32[2048,256]{1,0:T(8,128)S(1)} %bitcast.79, f32[]{:T(128)} %constant.14.clone.1, pred[2048]{0:T(1024)(128)(4,1)S(1)} %lt.72), kind=kCustom, calls=%fused_computation.12 | custom fusion | flops 1048576 | bytes 4196864 | tf_op jit(solution)/shard_map/scatter-add | solution.py:123
  163.4 2.7 convert_element_type.73
  166.1 74.5 %psum.23 = f32[256]{0:T(256)S(1)} all-reduce(f32[256]{0:T(256)S(1)} %get-tuple-element.17), channel_id=1, replica_groups=mesh['group'=8,'inner'=32] {'group','inner'}, use_global_device_ids=true, to_apply=%region_6.7 | all-reduce | flops 256 | bytes 2048 | tf_op jit(solution)/shard_map/psum | solution.py:104
  240.6 0.6 broadcast_multiply_fusion.2
  241.1 93.5 %all-reduce.3.cloned.1.call-done = (f32[256,256]{0,1:T(8,128)}, f32[256,256]{0,1:T(8,128)}) async-done(((f32[256,256]{0,1:T(8,128)}, f32[256,256]{0,1:T(8,128)}), (f32[256,256]{0,1:T(8,128)}, f32[256,256]{0,1:T(8,128)})) %all-reduce.3.cloned.1.call-update) | async-done | bytes 524304 | tf_op jit(solution)/shard_map/psum | solution.py:104
  334.6 1.1 broadcast_multiply_fusion
  335.7 0.8 copy.30
  336.6 0.8 copy.31
  (24 shorter events, 0.1 us)
Async XLA Ops:
  7.2 63.8 %copy-start = (bf16[256,256]{1,0:T(8,128)(2,1)S(1)}, bf16[256,256]{1,0:T(8,128)(2,1)}, u32[]{:S(2)}) copy-start(bf16[256,256]{1,0:T(8,128)(2,1)} %param.11) | copy-start | bytes 393220
  7.2 327.5 %all-reduce.3.cloned.1.call-start = ((), (), s32[]{:S(2)}) async-start(), calls=%async_computation | async-start | bytes 1048576 | tf_op jit(solution)/shard_map/psum | solution.py:104
  17.3 43.4 %copy-start.1 = (bf16[2048,256]{1,0:T(8,128)(2,1)S(1)}, bf16[2048,256]{1,0:T(8,128)(2,1)}, u32[]{:S(2)}) copy-start(bf16[2048,256]{1,0:T(8,128)(2,1)} %param.9) | copy-start | bytes 3145732
  60.6 1.5 copy-start.8
  60.7 2.4 copy-start.2
  62.1 1.3 copy-start.6
  68.8 2.3 copy-start.5
  68.8 2.5 copy-start.9
  68.8 2.5 copy-start.10
  73.5 1.2 copy-start.3
  104.4 1.9 copy-start.4
  106.3 1.8 copy-start.7
Sparse Core Ops, SparseCore 0:
  76.0 258.5 all-reduce.2

commit v2 on v0

v2 whole, which is shorter than its diff:
```python
import math

import jax
import jax.numpy as jnp
from jax import lax
from jax.experimental import pallas as pl
from jax.experimental.pallas import tpu as pltpu
from jax.sharding import PartitionSpec as P

MESH = pl.DeviceIdType.MESH
BF16, F32 = jnp.bfloat16, jnp.float32
ROWS, WIDTH, EDGE, TILES = 2048, 256, 128, 16
PARTS = 17
STEPS = (4, 3, 5, 2, 6, 1, 7, 0)


def dot(left, right):
    return jnp.dot(left, right, preferred_element_type=F32)


def dot_rows(left, right):
    return lax.dot_general(left, right, (((0,), (0,)), ((), ())), preferred_element_type=F32)


def dot_cols(left, right):
    return lax.dot_general(left, right, (((1,), (1,)), ((), ())), preferred_element_type=F32)


def to_blocks(rows):
    left = rows[:, :128].reshape(32, 8, 128)
    right = rows[:, 128:].reshape(32, 8, 128)
    return jnp.concatenate([left, right], axis=1).astype(BF16)


def from_blocks(blocks):
    wide = blocks.astype(F32)
    rows = jnp.concatenate([wide[:, :8], wide[:, 8:]], axis=2)
    return rows.reshape(256, 256).astype(BF16)


def kernel(
    idx_ref, ts_ref, bias_ref, ws_ref, wn_ref, feat_hbm, gout_hbm, adj_hbm,
    out_hbm, gf_hbm, gs_ref, gn_ref, gb_ref,
    feat, gout, adj, col, outb, halob, outg, retb, halo, adj1, at_own, at_halo, inv,
    s_own, p_self, mean, gpre, gagg, total, outv, gfv,
    part, r1buf, r1sum, r2buf, tiles, fin,
    lsem, s1, q1, s2, q2, sr, qr,
):
    g, j = lax.axis_index("group"), lax.axis_index("inner")
    z, y, cx, cc = j // 4, j % 4, g // 2, g % 2
    me = j * 8 + g

    load_feat = pltpu.make_async_copy(feat_hbm, feat, lsem.at[0])
    load_adj = pltpu.make_async_copy(adj_hbm, adj, lsem.at[1])
    load_gout = pltpu.make_async_copy(gout_hbm, gout, lsem.at[2])
    load_feat.start()
    load_adj.start()
    load_gout.start()

    barrier = pltpu.get_barrier_semaphore()

    def greet(t, carry):
        d = lax.rem(me + t, 256)
        pl.semaphore_signal(barrier, inc=1, device_id=(d % 8, d // 8), device_id_type=MESH)
        return carry

    lax.fori_loop(1, 256, greet, 0)

    turned = jnp.transpose(idx_ref[...].astype(F32)).astype(jnp.int32)
    for n in range(16):
        col[n] = jnp.broadcast_to(turned[:, n : n + 1], (128, 128))
    load_feat.wait()

    def pick(n, carry):
        slab = jnp.concatenate([col[2 * n], col[2 * n + 1]], axis=0)
        slab = jnp.concatenate([slab, slab], axis=1)
        lane = lax.broadcasted_iota(jnp.int32, (256, 256), 1)
        acc = jnp.zeros((256, 256), F32)
        for c in range(8):
            hot = jnp.where(slab == lane + 256 * c, 1.0, 0.0).astype(BF16)
            acc = acc + dot(hot, feat[2 * c : 2 * c + 2].reshape(256, 256))
        outb[pl.ds(n * 32, 32)] = to_blocks(acc)
        return carry

    lax.fori_loop(0, 8, pick, 0)
    own1 = pltpu.make_async_copy(outb.at[me], halob.at[me], lsem.at[3])
    own1.start()
    pl.semaphore_wait(barrier, 255)

    def send_plane(k, src, dst, ssem, rsem):
        dz = STEPS[k]

        def send(m, carry):
            h = ((cx + m // 8) % 4) * 2 + (cc + m // 4) % 2
            i = ((z + dz) % 8) * 4 + (y + m) % 4
            pltpu.make_async_remote_copy(
                src.at[i * 8 + h], dst.at[me], ssem.at[k], rsem.at[k], device_id=(h, i), device_id_type=MESH
            ).start()
            return carry

        lax.fori_loop(1 if dz == 0 else 0, 32, send, 0)

    def plane(k, src, dst, ssem, rsem):
        n = 31 if STEPS[k] == 0 else 32
        return pltpu.make_async_remote_copy(
            src.at[pl.ds(0, n)], dst.at[pl.ds(0, n)], ssem.at[k], rsem.at[k], device_id=(g, j), device_id_type=MESH
        )

    for k in range(8):
        send_plane(k, outb, halob, s1, q1)

    load_adj.wait()

    def prepare(b, carry):
        rows = pl.ds(pl.multiple_of(b * EDGE, EDGE), EDGE)
        a0 = adj[b, 0].astype(F32)
        a1 = adj[b, 1].astype(F32)
        degree = jnp.sum(a0 + a1, axis=1, keepdims=True)
        inv[rows, :] = jnp.broadcast_to(1.0 / jnp.maximum(degree, 1.0), (EDGE, EDGE))
        adj1[b] = a1.astype(BF16)
        t0 = ts_ref[b, 0]
        t1 = jnp.maximum(ts_ref[b, 1] - TILES, 0)
        block = feat[t0]
        s_own[rows, :] = dot(a0.astype(BF16), block)
        p_self[rows, :] = dot(feat[b], ws_ref[...]) + bias_ref[...]
        a0t = jnp.transpose(a0)
        a1t = jnp.transpose(a1)
        own = jnp.broadcast_to(t0, (EDGE, EDGE))
        far = jnp.broadcast_to(t1, (EDGE, EDGE))
        for e in range(TILES):
            at_own[e * EDGE : (e + 1) * EDGE, rows] = jnp.where(own == e, a0t, 0.0).astype(BF16)
            at_halo[e * EDGE : (e + 1) * EDGE, rows] = jnp.where(far == e, a1t, 0.0).astype(BF16)
        return carry

    lax.fori_loop(0, TILES, prepare, 0)
    load_gout.wait()

    own1.wait()
    for k in range(8):
        plane(k, outb, halob, s1, q1).wait_recv()
        n = (z + 8 - STEPS[k]) % 8
        halo[pl.ds(2 * n, 2)] = from_blocks(halob[pl.ds(n * 32, 32)]).reshape(2, EDGE, WIDTH)

    def layer(b, carry):
        rows = pl.ds(pl.multiple_of(b * 256, 256), 256)
        sums = []
        for u in range(2):
            t1 = jnp.maximum(ts_ref[2 * b + u, 1] - TILES, 0)
            block = halo[t1]
            sums.append(dot(adj1[2 * b + u], block))
        scale = inv[rows, :]
        scale = jnp.concatenate([scale, scale], axis=1)
        m = ((s_own[rows, :] + jnp.concatenate(sums, axis=0)) * scale).astype(BF16)
        mean[rows, :] = m
        pre = p_self[rows, :] + dot(m, wn_ref[...])
        sigma = 1.0 / (1.0 + jnp.exp(-pre))
        outv[rows, :] = (pre * sigma).astype(BF16)
        slope = sigma * (1.0 + pre * (1.0 - sigma))
        gp = (gout[rows, :].astype(F32) * slope).astype(BF16)
        gpre[rows, :] = gp
        gagg[rows, :] = (dot_cols(gp, wn_ref[...]) * scale).astype(BF16)
        return carry

    lax.fori_loop(0, 8, layer, 0)
    store_out = pltpu.make_async_copy(outv, out_hbm, lsem.at[4])
    store_out.start()

    for k in range(8):
        n = (z + STEPS[k]) % 8
        rows = pl.ds(pl.multiple_of(n * 256, 256), 256)
        acc = jnp.zeros((256, 256), F32)
        for c in range(8):
            acc = acc + dot(at_halo[rows, 256 * c : 256 * c + 256], gagg[256 * c : 256 * c + 256, :])
        outg[pl.ds(n * 32, 32)] = to_blocks(acc)
        send_plane(k, outg, retb, s2, q2)
    own2 = pltpu.make_async_copy(outg.at[me], retb.at[me], lsem.at[5])
    own2.start()

    def weights(c, carry):
        acc_self, acc_neigh, acc_bias = carry
        rows = pl.ds(pl.multiple_of(c * 256, 256), 256)
        gp = gpre[rows, :]
        acc_self = acc_self + dot_rows(feat[pl.ds(2 * c, 2)].reshape(256, 256), gp)
        acc_neigh = acc_neigh + dot_rows(mean[rows, :], gp)
        acc_bias = acc_bias + jnp.sum(gp.astype(F32).reshape(32, 8, 256), axis=0)
        return acc_self, acc_neigh, acc_bias

    zero = jnp.zeros((256, 256), F32)
    acc_self, acc_neigh, acc_bias = lax.fori_loop(0, 8, weights, (zero, zero, jnp.zeros((8, 256), F32)))
    bias_row = jnp.sum(acc_bias, axis=0, keepdims=True)
    bias_tile = jnp.concatenate([bias_row[:, :128], bias_row[:, 128:], jnp.zeros((6, 128), F32)], axis=0)
    for h in range(8):
        acc = acc_self if h < 4 else acc_neigh
        for a in range(8):
            r = (h % 4) * 64 + a * 8
            part[h, 2 * a] = acc[r : r + 8, :128]
            part[h, 2 * a + 1] = acc[r : r + 8, 128:]
        part[h, 16] = bias_tile

    def send_share(t, carry):
        h = (g + t) % 8
        pltpu.make_async_remote_copy(
            part.at[h], r1buf.at[g], sr.at[0], qr.at[0], device_id=(h, j), device_id_type=MESH
        ).start()
        return carry

    lax.fori_loop(1, 8, send_share, 0)
    r1buf[g] = part[g]

    def base(n, carry):
        rows = pl.ds(pl.multiple_of(n * 256, 256), 256)
        acc = dot_cols(gpre[rows, :], ws_ref[...])
        for c in range(8):
            acc = acc + dot(at_own[rows, 256 * c : 256 * c + 256], gagg[256 * c : 256 * c + 256, :])
        total[rows, :] = acc
        return carry

    lax.fori_loop(0, 8, base, 0)

    def settle(k):
        plane(k, outg, retb, s2, q2).wait_recv()
        n = (z + 8 - STEPS[k]) % 8
        rows = from_blocks(retb[pl.ds(n * 32, 32)])
        slots = jnp.concatenate([idx_ref[pl.ds(2 * n, 1), :], idx_ref[pl.ds(2 * n + 1, 1), :]], axis=1)
        slots = jnp.broadcast_to(slots, (256, 256))
        line = lax.broadcasted_iota(jnp.int32, (256, 256), 0)

        def add(c, carry):
            at = pl.ds(pl.multiple_of(c * 256, 256), 256)
            hot = jnp.where(slots == line + 256 * c, 1.0, 0.0).astype(BF16)
            total[at, :] += dot(hot, rows)
            return carry

        lax.fori_loop(0, 8, add, 0)

    def shares(n, sem, dst):
        return pltpu.make_async_remote_copy(
            dst.at[pl.ds(0, n)], dst.at[pl.ds(0, n)], sr.at[sem], qr.at[sem], device_id=(g, j), device_id_type=MESH
        )

    shares(7, 0, r1buf).wait_recv()
    r1sum[...] = r1buf[0]
    for h in range(1, 8):
        r1sum[...] += r1buf[h]

    def send_tile(t, carry):
        @pl.when(t != j)
        def _():
            pltpu.make_async_remote_copy(
                r1sum.at[t], r2buf.at[j], sr.at[1], qr.at[1], device_id=(g, t), device_id_type=MESH
            ).start()

        return carry

    lax.fori_loop(0, PARTS, send_tile, 0)

    settle(0)
    settle(1)

    @pl.when(j < PARTS)
    def _():
        r2buf[j] = r1sum[j]
        shares(31, 1, r2buf).wait_recv()
        acc = r2buf[0]
        for t in range(1, 32):
            acc = acc + r2buf[t]
        tiles[j] = acc

        def send_sum(t, carry):
            i = (j + t) % 32
            pltpu.make_async_remote_copy(
                tiles.at[j], tiles.at[j], sr.at[2], qr.at[2], device_id=(g, i), device_id_type=MESH
            ).start()
            return carry

        lax.fori_loop(1, 32, send_sum, 0)

    settle(2)
    settle(3)

    @pl.when(j < PARTS)
    def _():
        shares(PARTS - 1, 2, tiles).wait_recv()

    @pl.when(j >= PARTS)
    def _():
        shares(PARTS, 2, tiles).wait_recv()

    def send_all(t, carry):
        h = (g + t) % 8
        pltpu.make_async_remote_copy(
            tiles.at[pl.ds(0, 16)], fin.at[g], sr.at[3], qr.at[3], device_id=(h, j), device_id_type=MESH
        ).start()
        return carry

    lax.fori_loop(1, 8, send_all, 0)
    fin[g] = tiles[pl.ds(0, 16)]

    settle(4)
    settle(5)
    settle(6)
    own2.wait()
    settle(7)

    gfv[...] = total[...].astype(BF16)
    store_gf = pltpu.make_async_copy(gfv, gf_hbm, lsem.at[6])
    store_gf.start()

    factor = 1.0 / math.sqrt(ROWS * 256)
    shares(7, 3, fin).wait_recv()
    for h in range(8):
        ref = gs_ref if h < 4 else gn_ref
        for a in range(8):
            r = (h % 4) * 64 + a * 8
            ref[r : r + 8, :128] = fin[h, 2 * a] * factor
            ref[r : r + 8, 128:] = fin[h, 2 * a + 1] * factor
    gb_ref[:, :128] = tiles[16, 0:1] * factor
    gb_ref[:, 128:] = tiles[16, 1:2] * factor

    for k in range(8):
        plane(k, outb, halob, s1, q1).wait_send()
        plane(k, outg, retb, s2, q2).wait_send()
    shares(7, 0, r1buf).wait_send()

    @pl.when(j < PARTS)
    def _():
        shares(PARTS - 1, 1, r2buf).wait_send()
        shares(31, 2, r2buf).wait_send()

    @pl.when(j >= PARTS)
    def _():
        shares(PARTS, 1, r2buf).wait_send()

    shares(7, 3, fin).wait_send()
    store_out.wait()
    store_gf.wait()


def local(
    features, w_self, w_neigh, node_bias, grad_out, send_rows, send_count, adjacency, tile_source
):
    slot_rows = send_rows[0]
    keep = lax.broadcasted_iota(jnp.int32, slot_rows.shape, 2) < send_count[0][:, :, None]
    idx = jnp.where(keep, slot_rows, -1).reshape(16, 128)
    vmem, hbm = pl.BlockSpec(memory_space=pltpu.VMEM), pl.BlockSpec(memory_space=pl.ANY)
    tall = (ROWS, WIDTH)
    blocks = (256, 16, 128)
    dma = pltpu.SemaphoreType.DMA
    out, gf, gs, gn, gb = pl.pallas_call(
        kernel,
        out_shape=(
            jax.ShapeDtypeStruct(tall, BF16),
            jax.ShapeDtypeStruct(tall, BF16),
            jax.ShapeDtypeStruct((WIDTH, WIDTH), F32),
            jax.ShapeDtypeStruct((WIDTH, WIDTH), F32),
            jax.ShapeDtypeStruct((1, WIDTH), F32),
        ),
        in_specs=[vmem, pl.BlockSpec(memory_space=pltpu.SMEM), vmem, vmem, vmem, hbm, hbm, hbm],
        out_specs=(hbm, hbm, vmem, vmem, vmem),
        scratch_shapes=[
            pltpu.VMEM((TILES, EDGE, WIDTH), BF16),
            pltpu.VMEM(tall, BF16),
            pltpu.VMEM((TILES, 2, EDGE, EDGE), jnp.int32),
            pltpu.VMEM((16, 128, 128), jnp.int32),
            pltpu.VMEM(blocks, BF16),
            pltpu.VMEM(blocks, BF16),
            pltpu.VMEM(blocks, BF16),
            pltpu.VMEM(blocks, BF16),
            pltpu.VMEM((TILES, EDGE, WIDTH), BF16),
            pltpu.VMEM((TILES, EDGE, EDGE), BF16),
            pltpu.VMEM((ROWS, ROWS), BF16),
            pltpu.VMEM((ROWS, ROWS), BF16),
            pltpu.VMEM((ROWS, EDGE), F32),
            pltpu.VMEM(tall, F32),
            pltpu.VMEM(tall, F32),
            pltpu.VMEM(tall, BF16),
            pltpu.VMEM(tall, BF16),
            pltpu.VMEM(tall, BF16),
            pltpu.VMEM(tall, F32),
            pltpu.VMEM(tall, BF16),
            pltpu.VMEM(tall, BF16),
            pltpu.VMEM((8, PARTS, 8, 128), F32),
            pltpu.VMEM((8, PARTS, 8, 128), F32),
            pltpu.VMEM((PARTS, 8, 128), F32),
            pltpu.VMEM((32, 8, 128), F32),
            pltpu.VMEM((PARTS, 8, 128), F32),
            pltpu.VMEM((8, 16, 8, 128), F32),
            dma((7,)),
            dma((8,)),
            dma((8,)),
            dma((8,)),
            dma((8,)),
            dma((4,)),
            dma((4,)),
        ],
        compiler_params=pltpu.CompilerParams(
            collective_id=0, has_side_effects=True, vmem_limit_bytes=56 << 20
        ),
        name="sage_layer",
    )(
        idx, tile_source[0], node_bias.reshape(1, WIDTH), w_self, w_neigh, features.reshape(TILES, EDGE, WIDTH), grad_out, adjacency[0]
    )
    return out, gf, gs, gn, gb.reshape(WIDTH)


def solution(mesh):
    rows = P(("group", "inner"), None)
    placed = (
        rows,
        P(),
        P(),
        P(),
        rows,
        P(("group", "inner"), None, None, None),
        P(("group", "inner"), None, None),
        P(("group", "inner"), None, None, None, None),
        P(("group", "inner"), None, None),
    )
    return jax.shard_map(
        local, mesh=mesh, in_specs=placed, out_specs=(rows, rows, P(), P(), P()), check_vma=False
    )
```

time: 443 us -> 111 us (0.25)
  waiting for transfers between devices: 218 us -> 0 us
  Pallas kernels: 0 us -> 101 us
  blocking collectives: 97.3 us -> 0 us
  other arithmetic: 31.5 us -> 0.71 us
  local copies, waits for them, and re-layouts: 36.4 us -> 8.54 us
  starting transfers between devices: 26 us -> 0 us
  matrix products: 18 us -> 0 us
  between operations: 14.2 us -> 0.68 us
    psum x1 -> x0, waiting for transfers between devices: 172 us -> none  [local(): lax.psum((part_self, part_neigh, part_bias), ('group', 'inner'))]
    pallas_call x0 -> x1, Pallas kernels: none -> 101 us  [local(): pl.pallas_call(kernel, out_shape=(jax.ShapeDtypeStruct(tall, BF16), jax.S...]
    psum x1 -> x0, blocking collectives: 76.6 us -> none  [local(): lax.psum((part_self, part_neigh, part_bias), ('group', 'inner'))]
    all_to_all x3 -> x0, waiting for transfers between devices: 45.8 us -> none  [the longest x1 23.2 us: local(): lax.all_to_all(sectioned, 'inner', split_axis=0, concat_axis=0, tiled=True)]
    all_to_all x3 -> x0, starting transfers between devices: 26 us -> none  [the longest x1 11.4 us: local(): lax.all_to_all(sectioned, 'inner', split_axis=0, concat_axis=0, tiled=True)]
    scatter-add x2 -> x0, other arithmetic: 22.9 us -> none  [the longest x1 12.9 us: local(): grad_total.at[slot_rows.reshape(-1)].add(masked.reshape(-1, width))]
    all_to_all x1 -> x0, blocking collectives: 20.7 us -> none  [local(): lax.all_to_all(outgoing, 'group', split_axis=1, concat_axis=1, tiled=True)]
    dot_general x8 -> x0, matrix products: 18 us -> none  [the longest x1 4.26 us: local(): jnp.einsum('dkrc,drh->dkch', adj_values, back_agg, preferred_element_type...]
  transfers between devices with their start and end apart: 4 -> 0, of which waited for: 3 -> 0; matrix products, arithmetic and copies ran while one was open for 3% -> 0% of each run, Pallas kernels for 0% -> 0%
where the time goes in v2:
time: 111 us
  Pallas kernels  101 us (91%)
  local copies, waits for them, and re-layouts  8.54 us (8%)
    pallas_call x1, Pallas kernels, local(): pl.pallas_call(kernel, out_shape=(jax.ShapeDtypeStruct(tall, BF16), jax.S...  101 us
    unnamed x14, local copies, waits for them, and re-layouts  6.2 us

profile of v2, /device:TPU:1, one launch (start us, length us, event | category | flops | bytes accessed | tf_op | source)
XLA Modules:
  0.0 110.8 jit_solution(3645078887176804440)
XLA Ops:
  0.6 1.4 %copy.19.ts_ref = s32[16,2]{1,0:T(8,128)} copy(s32[16,2]{0,1:T(2,128)} %bitcast.12) | data formatting | bytes 256 | tf_op jit(solution)/shard_map/squeeze | solution.py:401
  2.0 0.8 copy.17
  2.7 0.1 iota_compare_fusion
  2.9 0.1 lt.17
  3.0 0.9 copy.18
  3.8 0.1 squeeze.9
  4.0 0.6 broadcast_select_fusion.idx_ref
  4.6 100.9 %sage_layer.1 = (bf16[2048,256]{1,0:T(8,128)(2,1)}, bf16[2048,256]{1,0:T(8,128)(2,1)}, f32[256,256]{1,0:T(8,128)}, f32[256,256]{1,0:T(8,128)}, f32[1,256]{1,0:T(1,128)}) custom-call(s32[16,128]{1,0:T(8,128)} %broadcast_select_fusion.idx_ref, s32[16,2]{1,0:T(8,128)} %copy.19.ts_ref, f32[1,256]{1,0:T(1,128)} %bitcast.11, bf16[256,256]{1,0:T(8,128)(2,1)} %ws_ref.1, ...), custom_call_target="tpu_custom_call" | custom-call | tf_op jit(solution)/shard_map/sage_layer/pallas_call | solution.py:349
  105.4 0.0 copy-start
  105.4 0.0 copy-start.2
  105.5 0.0 copy-start.1
  105.5 2.4 %copy.25 = bf16[2048,256]{1,0:T(8,128)(2,1)} copy(bf16[2048,256]{1,0:T(8,128)(2,1)} %get-tuple-element.20) | data formatting | bytes 2097152
  107.8 0.0 copy-done
  107.8 0.0 copy-start.3
  107.8 1.0 copy.26
  108.8 0.0 copy-done.2
  108.8 0.7 copy.27
  109.5 0.0 copy-done.1
  109.5 0.7 copy.28
  110.2 0.0 copy-done.3
  110.2 0.6 copy.29
Async XLA Ops:
  105.4 2.4 %copy-start = (bf16[2048,256]{1,0:T(8,128)(2,1)S(1)}, bf16[2048,256]{1,0:T(8,128)(2,1)}, u32[]{:S(2)}) copy-start(bf16[2048,256]{1,0:T(8,128)(2,1)} %get-tuple-element.21) | copy-start | bytes 3145732
  105.4 3.4 %copy-start.2 = (f32[256,256]{1,0:T(8,128)S(1)}, f32[256,256]{1,0:T(8,128)}, u32[]{:S(2)}) copy-start(f32[256,256]{1,0:T(8,128)} %get-tuple-element.22) | copy-start | bytes 786436
  105.5 4.1 %copy-start.1 = (f32[256,256]{1,0:T(8,128)S(1)}, f32[256,256]{1,0:T(8,128)}, u32[]{:S(2)}) copy-start(f32[256,256]{1,0:T(8,128)} %get-tuple-element.23) | copy-start | bytes 786436
  107.8 2.4 %copy-start.3 = (f32[1,256]{1,0:T(1,128)S(1)}, f32[1,256]{1,0:T(1,128)}, u32[]{:S(2)}) copy-start(f32[1,256]{1,0:T(1,128)} %get-tuple-element.14) | copy-start | bytes 3076

commit v3 on v2

--- a/solution.py
+++ b/solution.py
@@ -39,11 +39,11 @@
 
 
 def kernel(
-    idx_ref, ts_ref, bias_ref, ws_ref, wn_ref, feat_hbm, gout_hbm, adj_hbm,
+    slots_ref, count_ref, ts_ref, bias_ref, ws_ref, wn_ref, feat_hbm, gout_hbm, adj_hbm,
     out_hbm, gf_hbm, gs_ref, gn_ref, gb_ref,
     feat, gout, adj, col, outb, halob, outg, retb, halo, adj1, at_own, at_halo, inv,
     s_own, p_self, mean, gpre, gagg, total, outv, gfv,
-    part, r1buf, r1sum, r2buf, tiles, fin,
+    oht, lanes, part, r1buf, r1sum, r2buf, tiles, fin,
     lsem, s1, q1, s2, q2, sr, qr,
 ):
     g, j = lax.axis_index("group"), lax.axis_index("inner")
@@ -66,25 +66,27 @@
 
     lax.fori_loop(1, 256, greet, 0)
 
-    turned = jnp.transpose(idx_ref[...].astype(F32)).astype(jnp.int32)
+    live = lax.broadcasted_iota(jnp.int32, (8, 8, 32), 1) < count_ref[...][:, None, :]
+    index = jnp.where(live, slots_ref[...], -1).reshape(64, 32)
+    for i in range(32):
+        col[i] = jnp.broadcast_to(index[:, i : i + 1], (64, 128)).astype(jnp.int16)
+    turned = jnp.transpose(index)
     for n in range(16):
-        col[n] = jnp.broadcast_to(turned[:, n : n + 1], (128, 128))
+        lanes[n : n + 1, :] = jnp.concatenate([turned[2 * n : 2 * n + 1], turned[2 * n + 1 : 2 * n + 2]], axis=1)
     load_feat.wait()
 
-    def pick(n, carry):
-        slab = jnp.concatenate([col[2 * n], col[2 * n + 1]], axis=0)
-        slab = jnp.concatenate([slab, slab], axis=1)
-        lane = lax.broadcasted_iota(jnp.int32, (256, 256), 1)
+    def pick(k):
+        n = (z + STEPS[k]) % 8
+        slab = col[pl.ds(4 * n, 4)].reshape(256, 128)
+        lane = lax.broadcasted_iota(jnp.int32, (256, 128), 1)
         acc = jnp.zeros((256, 256), F32)
         for c in range(8):
-            hot = jnp.where(slab == lane + 256 * c, 1.0, 0.0).astype(BF16)
+            halves = [slab == (lane + 256 * c + 128 * u).astype(jnp.int16) for u in range(2)]
+            hot = jnp.concatenate([jnp.where(half, BF16(1), BF16(0)) for half in halves], axis=1)
             acc = acc + dot(hot, feat[2 * c : 2 * c + 2].reshape(256, 256))
         outb[pl.ds(n * 32, 32)] = to_blocks(acc)
-        return carry
-
-    lax.fori_loop(0, 8, pick, 0)
-    own1 = pltpu.make_async_copy(outb.at[me], halob.at[me], lsem.at[3])
-    own1.start()
+
+    pick(0)
     pl.semaphore_wait(barrier, 255)
 
     def send_plane(k, src, dst, ssem, rsem):
@@ -107,7 +109,11 @@
         )
 
     for k in range(8):
+        if k:
+            pick(k)
         send_plane(k, outb, halob, s1, q1)
+    own1 = pltpu.make_async_copy(outb.at[me], halob.at[me], lsem.at[3])
+    own1.start()
 
     load_adj.wait()
 
@@ -118,8 +124,8 @@
         degree = jnp.sum(a0 + a1, axis=1, keepdims=True)
         inv[rows, :] = jnp.broadcast_to(1.0 / jnp.maximum(degree, 1.0), (EDGE, EDGE))
         adj1[b] = a1.astype(BF16)
-        t0 = ts_ref[b, 0]
-        t1 = jnp.maximum(ts_ref[b, 1] - TILES, 0)
+        t0 = ts_ref[0, b]
+        t1 = jnp.maximum(ts_ref[1, b] - TILES, 0)
         block = feat[t0]
         s_own[rows, :] = dot(a0.astype(BF16), block)
         p_self[rows, :] = dot(feat[b], ws_ref[...]) + bias_ref[...]
@@ -133,6 +139,17 @@
         return carry
 
     lax.fori_loop(0, TILES, prepare, 0)
+
+    def spread(n, carry):
+        slots = jnp.concatenate([lanes[pl.ds(2 * n, 1), :], lanes[pl.ds(2 * n + 1, 1), :]], axis=1)
+        line = lax.broadcasted_iota(jnp.int32, (256, 256), 0).astype(jnp.int16)
+        for c in range(8):
+            here = jnp.broadcast_to(slots - 256 * c, (256, 256)).astype(jnp.int16)
+            hot = jnp.where(here == line, BF16(1), BF16(0))
+            oht[256 * c : 256 * c + 256, pl.ds(pl.multiple_of(n * 256, 256), 256)] = hot
+        return carry
+
+    lax.fori_loop(0, 8, spread, 0)
     load_gout.wait()
 
     own1.wait()
@@ -145,7 +162,7 @@
         rows = pl.ds(pl.multiple_of(b * 256, 256), 256)
         sums = []
         for u in range(2):
-            t1 = jnp.maximum(ts_ref[2 * b + u, 1] - TILES, 0)
+            t1 = jnp.maximum(ts_ref[1, 2 * b + u] - TILES, 0)
             block = halo[t1]
             sums.append(dot(adj1[2 * b + u], block))
         scale = inv[rows, :]
@@ -161,11 +178,11 @@
         gagg[rows, :] = (dot_cols(gp, wn_ref[...]) * scale).astype(BF16)
         return carry
 
-    lax.fori_loop(0, 8, layer, 0)
+    lax.fori_loop(0, 8, layer, 0, unroll=2)
     store_out = pltpu.make_async_copy(outv, out_hbm, lsem.at[4])
     store_out.start()
 
-    for k in range(8):
+    def give_back(k):
         n = (z + STEPS[k]) % 8
         rows = pl.ds(pl.multiple_of(n * 256, 256), 256)
         acc = jnp.zeros((256, 256), F32)
@@ -173,8 +190,9 @@
             acc = acc + dot(at_halo[rows, 256 * c : 256 * c + 256], gagg[256 * c : 256 * c + 256, :])
         outg[pl.ds(n * 32, 32)] = to_blocks(acc)
         send_plane(k, outg, retb, s2, q2)
-    own2 = pltpu.make_async_copy(outg.at[me], retb.at[me], lsem.at[5])
-    own2.start()
+
+    for k in range(3):
+        give_back(k)
 
     def weights(c, carry):
         acc_self, acc_neigh, acc_bias = carry
@@ -207,6 +225,49 @@
     lax.fori_loop(1, 8, send_share, 0)
     r1buf[g] = part[g]
 
+    for k in range(3, 8):
+        give_back(k)
+    own2 = pltpu.make_async_copy(outg.at[me], retb.at[me], lsem.at[5])
+    own2.start()
+
+    def settle(ks, last=False):
+        planes, spots = [], []
+        for k in ks:
+            plane(k, outg, retb, s2, q2).wait_recv()
+            n = (z + 8 - STEPS[k]) % 8
+            planes.append(from_blocks(retb[pl.ds(n * 32, 32)]))
+            spots.append(pl.ds(pl.multiple_of(n * 256, 256), 256))
+        for c in range(8):
+            at = slice(256 * c, 256 * c + 256)
+            acc = total[at, :]
+            for spot, rows in zip(spots, planes):
+                acc = acc + dot(oht[at, spot], rows)
+            if last:
+                gfv[at, :] = acc.astype(BF16)
+            else:
+                total[at, :] = acc
+
+    def shares(n, sem, dst):
+        return pltpu.make_async_remote_copy(
+            dst.at[pl.ds(0, n)], dst.at[pl.ds(0, n)], sr.at[sem], qr.at[sem], device_id=(g, j), device_id_type=MESH
+        )
+
+    shares(7, 0, r1buf).wait_recv()
+    r1sum[...] = r1buf[0]
+    for h in range(1, 8):
+        r1sum[...] += r1buf[h]
+
+    def send_tile(t, carry):
+        @pl.when(t != j)
+        def _():
+            pltpu.make_async_remote_copy(
+                r1sum.at[t], r2buf.at[j], sr.at[1], qr.at[1], device_id=(g, t), device_id_type=MESH
+            ).start()
+
+        return carry
+
+    lax.fori_loop(0, PARTS, send_tile, 0)
+
     def base(n, carry):
         rows = pl.ds(pl.multiple_of(n * 256, 256), 256)
         acc = dot_cols(gpre[rows, :], ws_ref[...])
@@ -217,45 +278,6 @@
 
     lax.fori_loop(0, 8, base, 0)
 
-    def settle(k):
-        plane(k, outg, retb, s2, q2).wait_recv()
-        n = (z + 8 - STEPS[k]) % 8
-        rows = from_blocks(retb[pl.ds(n * 32, 32)])
-        slots = jnp.concatenate([idx_ref[pl.ds(2 * n, 1), :], idx_ref[pl.ds(2 * n + 1, 1), :]], axis=1)
-        slots = jnp.broadcast_to(slots, (256, 256))
-        line = lax.broadcasted_iota(jnp.int32, (256, 256), 0)
-
-        def add(c, carry):
-            at = pl.ds(pl.multiple_of(c * 256, 256), 256)
-            hot = jnp.where(slots == line + 256 * c, 1.0, 0.0).astype(BF16)
-            total[at, :] += dot(hot, rows)
-            return carry
-
-        lax.fori_loop(0, 8, add, 0)
-
-    def shares(n, sem, dst):
-        return pltpu.make_async_remote_copy(
-            dst.at[pl.ds(0, n)], dst.at[pl.ds(0, n)], sr.at[sem], qr.at[sem], device_id=(g, j), device_id_type=MESH
-        )
-
-    shares(7, 0, r1buf).wait_recv()
-    r1sum[...] = r1buf[0]
-    for h in range(1, 8):
-        r1sum[...] += r1buf[h]
-
-    def send_tile(t, carry):
-        @pl.when(t != j)
-        def _():
-            pltpu.make_async_remote_copy(
-                r1sum.at[t], r2buf.at[j], sr.at[1], qr.at[1], device_id=(g, t), device_id_type=MESH
-            ).start()
-
-        return carry
-
-    lax.fori_loop(0, PARTS, send_tile, 0)
-
-    settle(0)
-    settle(1)
 
     @pl.when(j < PARTS)
     def _():
@@ -275,8 +297,8 @@
 
         lax.fori_loop(1, 32, send_sum, 0)
 
-    settle(2)
-    settle(3)
+    settle((0,))
+    settle((1, 2))
 
     @pl.when(j < PARTS)
     def _():
@@ -296,13 +318,10 @@
     lax.fori_loop(1, 8, send_all, 0)
     fin[g] = tiles[pl.ds(0, 16)]
 
-    settle(4)
-    settle(5)
-    settle(6)
+    settle((3, 4))
+    settle((5, 6))
     own2.wait()
-    settle(7)
-
-    gfv[...] = total[...].astype(BF16)
+    settle((7,), True)
     store_gf = pltpu.make_async_copy(gfv, gf_hbm, lsem.at[6])
     store_gf.start()
 
@@ -336,17 +355,27 @@
     store_gf.wait()
 
 
+def hand_over(*refs):
+    held, sems = refs[10:15], refs[15]
+    taken = [pltpu.make_async_copy(refs[n], held[n], sems.at[n]) for n in range(5)]
+    given = [pltpu.make_async_copy(held[n], refs[5 + n], sems.at[5 + n]) for n in range(5)]
+    for copy in taken:
+        copy.start()
+    for n in range(5):
+        taken[n].wait()
+        given[n].start()
+    for copy in given:
+        copy.wait()
+
+
 def local(
     features, w_self, w_neigh, node_bias, grad_out, send_rows, send_count, adjacency, tile_source
 ):
-    slot_rows = send_rows[0]
-    keep = lax.broadcasted_iota(jnp.int32, slot_rows.shape, 2) < send_count[0][:, :, None]
-    idx = jnp.where(keep, slot_rows, -1).reshape(16, 128)
     vmem, hbm = pl.BlockSpec(memory_space=pltpu.VMEM), pl.BlockSpec(memory_space=pl.ANY)
     tall = (ROWS, WIDTH)
     blocks = (256, 16, 128)
     dma = pltpu.SemaphoreType.DMA
-    out, gf, gs, gn, gb = pl.pallas_call(
+    made = pl.pallas_call(
         kernel,
         out_shape=(
             jax.ShapeDtypeStruct(tall, BF16),
@@ -355,13 +384,13 @@
             jax.ShapeDtypeStruct((WIDTH, WIDTH), F32),
             jax.ShapeDtypeStruct((1, WIDTH), F32),
         ),
-        in_specs=[vmem, pl.BlockSpec(memory_space=pltpu.SMEM), vmem, vmem, vmem, hbm, hbm, hbm],
+        in_specs=[vmem, vmem, pl.BlockSpec(memory_space=pltpu.SMEM), vmem, vmem, vmem, hbm, hbm, hbm],
         out_specs=(hbm, hbm, vmem, vmem, vmem),
         scratch_shapes=[
             pltpu.VMEM((TILES, EDGE, WIDTH), BF16),
             pltpu.VMEM(tall, BF16),
             pltpu.VMEM((TILES, 2, EDGE, EDGE), jnp.int32),
-            pltpu.VMEM((16, 128, 128), jnp.int32),
+            pltpu.VMEM((32, 64, 128), jnp.int16),
             pltpu.VMEM(blocks, BF16),
             pltpu.VMEM(blocks, BF16),
             pltpu.VMEM(blocks, BF16),
@@ -379,6 +408,8 @@
             pltpu.VMEM(tall, F32),
             pltpu.VMEM(tall, BF16),
             pltpu.VMEM(tall, BF16),
+            pltpu.VMEM((ROWS, ROWS), BF16),
+            pltpu.VMEM((16, 128), jnp.int32),
             pltpu.VMEM((8, PARTS, 8, 128), F32),
             pltpu.VMEM((8, PARTS, 8, 128), F32),
             pltpu.VMEM((PARTS, 8, 128), F32),
@@ -398,8 +429,17 @@
         ),
         name="sage_layer",
     )(
-        idx, tile_source[0], node_bias.reshape(1, WIDTH), w_self, w_neigh, features.reshape(TILES, EDGE, WIDTH), grad_out, adjacency[0]
+        send_rows[0].transpose(1, 2, 0), send_count[0].T, tile_source[0].T, node_bias.reshape(1, WIDTH), w_self, w_neigh, features.reshape(TILES, EDGE, WIDTH), grad_out, adjacency[0]
     )
+    out, gf, gs, gn, gb = pl.pallas_call(
+        hand_over,
+        out_shape=[jax.ShapeDtypeStruct(a.shape, a.dtype) for a in made],
+        in_specs=[hbm] * 5,
+        out_specs=[hbm] * 5,
+        scratch_shapes=[pltpu.VMEM(a.shape, a.dtype) for a in made] + [dma((10,))],
+        compiler_params=pltpu.CompilerParams(vmem_limit_bytes=60 << 20),
+        name="hand_over",
+    )(*made)
     return out, gf, gs, gn, gb.reshape(WIDTH)
 
 

time: 111 us -> 95.5 us (0.86)
  local copies, waits for them, and re-layouts: 8.54 us -> 0 us
  Pallas kernels: 101 us -> 94.8 us
    pallas_call x1, Pallas kernels: 101 us -> 92 us  [local(): pl.pallas_call(kernel, out_shape=(jax.ShapeDtypeStruct(tall, BF16), jax.S...]
    unnamed x14 -> x0, local copies, waits for them, and re-layouts: 6.2 us -> none
    pallas_call x0 -> x1, Pallas kernels: none -> 2.79 us  [local(): pl.pallas_call(hand_over, out_shape=[jax.ShapeDtypeStruct(a.shape, a.dtyp...]
    squeeze x2 -> x0, local copies, waits for them, and re-layouts: 1.46 us -> none  [the longest x1 1.35 us: local(): tile_source[0]]
where the time goes in v3:
time: 95.5 us; the launch traced here: 95.4 us
  Pallas kernels  94.8 us (99%)
    pallas_call x1, Pallas kernels, local(): pl.pallas_call(kernel, out_shape=(jax.ShapeDtypeStruct(tall, BF16), jax.S...  92 us
    pallas_call x1, Pallas kernels, local(): pl.pallas_call(hand_over, out_shape=[jax.ShapeDtypeStruct(a.shape, a.dtyp...  2.79 us

profile of v3, /device:TPU:1, one launch (start us, length us, event | category | flops | bytes accessed | tf_op | source)
XLA Modules:
  0.0 95.4 jit_solution(4988451086580311450)
XLA Ops:
  0.6 92.0 %sage_layer.1 = (bf16[2048,256]{1,0:T(8,128)(2,1)}, bf16[2048,256]{1,0:T(8,128)(2,1)}, f32[256,256]{1,0:T(8,128)}, f32[256,256]{1,0:T(8,128)}, f32[1,256]{1,0:T(1,128)}) custom-call(s32[8,8,32]{2,1,0:T(8,128)} %bitcast.15, s32[8,32]{1,0:T(8,128)} %bitcast.16, s32[2,16]{1,0:T(2,128)} %bitcast.17, f32[1,256]{1,0:T(1,128)} %bitcast.18, ...), custom_call_target="tpu_custom_call" | custom-call | tf_op jit(solution)/shard_map/sage_layer/pallas_call | solution.py:378
  92.6 2.8 %hand_over.1 = (bf16[2048,256]{1,0:T(8,128)(2,1)}, bf16[2048,256]{1,0:T(8,128)(2,1)}, f32[256,256]{1,0:T(8,128)}, f32[256,256]{1,0:T(8,128)}, f32[1,256]{1,0:T(1,128)}) custom-call(bf16[2048,256]{1,0:T(8,128)(2,1)} %get-tuple-element.15.refs_0_, bf16[2048,256]{1,0:T(8,128)(2,1)} %get-tuple-element.16.refs_1_, f32[256,256]{1,0:T(8,128)} %get-tuple-element.17.refs_2_, ...), custom_call_target="tpu_custom_call" | custom-call | tf_op jit(solution)/shard_map/hand_over/pallas_call | solution.py:434

commit v4 on v3

v4 whole, which is shorter than its diff:
```python
import math

import jax
import jax.numpy as jnp
from jax import lax
from jax.experimental import pallas as pl
from jax.experimental.pallas import tpu as pltpu
from jax.sharding import PartitionSpec as P

FLAT = pl.DeviceIdType.LOGICAL
BF16, F32 = jnp.bfloat16, jnp.float32
ROWS, WIDTH, EDGE, TILES = 2048, 256, 128, 16
OWNERS = 32
ROUNDS = ((4,), (3, 5), (2, 6), (1, 7), (0,))


def dot(left, right):
    return jnp.dot(left, right, preferred_element_type=F32)


def dot_rows(left, right):
    return lax.dot_general(left, right, (((0,), (0,)), ((), ())), preferred_element_type=F32)


def dot_cols(left, right):
    return lax.dot_general(left, right, (((1,), (1,)), ((), ())), preferred_element_type=F32)


def to_blocks(rows):
    left = rows[:, :128].reshape(32, 8, 128)
    right = rows[:, 128:].reshape(32, 8, 128)
    return jnp.concatenate([left, right], axis=1).astype(BF16)


def from_blocks(blocks):
    wide = blocks.astype(F32)
    rows = jnp.concatenate([wide[:, :8], wide[:, 8:]], axis=2)
    return rows.reshape(256, 256).astype(BF16)


def kernel(
    slots_ref, count_ref, ts_ref, bias_ref, ws_ref, wn_ref, feat_hbm, gout_hbm, adj_hbm,
    out_ref, gf_ref, gs_ref, gn_ref, gb_ref,
    feat, gout, adj, col, outb, halob, outg, retb, halo, adj1, at_own, at_halo, inv,
    s_own, p_self, mean, gpre, gagg, total,
    oht, lanes, part, shares, layers, done, b_shares, b_layers, b_done,
    lsem, s1, q1, s2, q2, sr, qr,
):
    g, j = lax.axis_index("group"), lax.axis_index("inner")
    z, y, cx, cc = j // 4, j % 4, g // 2, g % 2
    me, flat = j * 8 + g, g * 32 + j

    load_feat = pltpu.make_async_copy(feat_hbm, feat, lsem.at[0])
    load_adj = pltpu.make_async_copy(adj_hbm, adj, lsem.at[1])
    load_gout = pltpu.make_async_copy(gout_hbm, gout, lsem.at[2])
    load_feat.start()
    load_adj.start()
    load_gout.start()

    barrier = pltpu.get_barrier_semaphore()

    def greet(t, carry):
        d = lax.rem(flat + t, 256)
        pl.semaphore_signal(barrier, inc=1, device_id=d, device_id_type=FLAT)
        return carry

    lax.fori_loop(1, 256, greet, 0, unroll=5)

    live = lax.broadcasted_iota(jnp.int32, (8, 8, 32), 1) < count_ref[...][:, None, :]
    index = jnp.where(live, slots_ref[...], -1).reshape(64, 32)
    for i in range(32):
        col[i] = jnp.broadcast_to(index[:, i : i + 1], (64, 128)).astype(jnp.int16)
    turned = jnp.transpose(index)
    for n in range(16):
        lanes[n : n + 1, :] = jnp.concatenate([turned[2 * n : 2 * n + 1], turned[2 * n + 1 : 2 * n + 2]], axis=1)
    load_feat.wait()

    def pick(dz):
        n = (z + dz) % 8
        slab = col[pl.ds(4 * n, 4)].reshape(256, 128)
        lane = lax.broadcasted_iota(jnp.int32, (256, 128), 1)
        acc = jnp.zeros((256, 256), F32)
        for c in range(8):
            halves = [slab == (lane + 256 * c + 128 * u).astype(jnp.int16) for u in range(2)]
            hot = jnp.concatenate([jnp.where(half, BF16(1), BF16(0)) for half in halves], axis=1)
            acc = acc + dot(hot, feat[2 * c : 2 * c + 2].reshape(256, 256))
        outb[pl.ds(n * 32, 32)] = to_blocks(acc)

    pick(ROUNDS[0][0])
    pl.semaphore_wait(barrier, 255)

    def send_round(steps, src, dst, ssem, rsem):
        def send(m, carry):
            h = ((cx + m // 8) % 4) * 2 + (cc + m // 4) % 2
            for dz in steps:
                i = ((z + dz) % 8) * 4 + (y + m) % 4
                pltpu.make_async_remote_copy(
                    src.at[i * 8 + h], dst.at[me], ssem.at[dz], rsem.at[dz], device_id=h * 32 + i, device_id_type=FLAT
                ).start()
            return carry

        if steps[0] == 0:
            lax.fori_loop(1, 32, send, 0)
        else:
            lax.fori_loop(0, 32, send, 0, unroll=2)

    def plane(dz, src, dst, ssem, rsem):
        n = 32 if dz else 31
        return pltpu.make_async_remote_copy(
            src.at[pl.ds(0, n)], dst.at[pl.ds(0, n)], ssem.at[dz], rsem.at[dz], device_id=flat, device_id_type=FLAT
        )

    for steps in ROUNDS:
        for dz in steps:
            if dz != ROUNDS[0][0]:
                pick(dz)
        send_round(steps, outb, halob, s1, q1)
    own1 = pltpu.make_async_copy(outb.at[me], halob.at[me], lsem.at[3])
    own1.start()

    load_adj.wait()

    def prepare(b, carry):
        rows = pl.ds(pl.multiple_of(b * EDGE, EDGE), EDGE)
        a0 = adj[b, 0].astype(F32)
        a1 = adj[b, 1].astype(F32)
        degree = jnp.sum(a0 + a1, axis=1, keepdims=True)
        inv[rows, :] = jnp.broadcast_to(1.0 / jnp.maximum(degree, 1.0), (EDGE, EDGE))
        adj1[b] = a1.astype(BF16)
        t0 = ts_ref[0, b]
        t1 = jnp.maximum(ts_ref[1, b] - TILES, 0)
        block = feat[t0]
        s_own[rows, :] = dot(a0.astype(BF16), block)
        p_self[rows, :] = dot(feat[b], ws_ref[...]) + bias_ref[...]
        a0t = jnp.transpose(a0)
        a1t = jnp.transpose(a1)
        own = jnp.broadcast_to(t0, (EDGE, EDGE))
        far = jnp.broadcast_to(t1, (EDGE, EDGE))
        for e in range(TILES):
            at_own[e * EDGE : (e + 1) * EDGE, rows] = jnp.where(own == e, a0t, 0.0).astype(BF16)
            at_halo[e * EDGE : (e + 1) * EDGE, rows] = jnp.where(far == e, a1t, 0.0).astype(BF16)
        return carry

    lax.fori_loop(0, TILES, prepare, 0)

    def spread(n, carry):
        slots = jnp.concatenate([lanes[pl.ds(2 * n, 1), :], lanes[pl.ds(2 * n + 1, 1), :]], axis=1)
        line = lax.broadcasted_iota(jnp.int32, (256, 256), 0).astype(jnp.int16)
        for c in range(8):
            here = jnp.broadcast_to(slots - 256 * c, (256, 256)).astype(jnp.int16)
            hot = jnp.where(here == line, BF16(1), BF16(0))
            oht[256 * c : 256 * c + 256, pl.ds(pl.multiple_of(n * 256, 256), 256)] = hot
        return carry

    lax.fori_loop(0, 8, spread, 0)
    load_gout.wait()

    own1.wait()
    for steps in ROUNDS:
        for dz in steps:
            plane(dz, outb, halob, s1, q1).wait_recv()
            n = (z + 8 - dz) % 8
            halo[pl.ds(2 * n, 2)] = from_blocks(halob[pl.ds(n * 32, 32)]).reshape(2, EDGE, WIDTH)

    def layer(b, carry):
        rows = pl.ds(pl.multiple_of(b * 256, 256), 256)
        sums = []
        for u in range(2):
            t1 = jnp.maximum(ts_ref[1, 2 * b + u] - TILES, 0)
            block = halo[t1]
            sums.append(dot(adj1[2 * b + u], block))
        scale = inv[rows, :]
        scale = jnp.concatenate([scale, scale], axis=1)
        m = ((s_own[rows, :] + jnp.concatenate(sums, axis=0)) * scale).astype(BF16)
        mean[rows, :] = m
        pre = p_self[rows, :] + dot(m, wn_ref[...])
        sigma = 0.5 + 0.5 * jnp.tanh(0.5 * pre)
        out_ref[rows, :] = (pre * sigma).astype(BF16)
        slope = sigma * (1.0 + pre * (1.0 - sigma))
        gp = (gout[rows, :].astype(F32) * slope).astype(BF16)
        gpre[rows, :] = gp
        gagg[rows, :] = (dot_cols(gp, wn_ref[...]) * scale).astype(BF16)
        return carry

    lax.fori_loop(0, 8, layer, 0, unroll=4)

    def give_back(steps):
        for dz in steps:
            n = (z + dz) % 8
            rows = pl.ds(pl.multiple_of(n * 256, 256), 256)
            acc = jnp.zeros((256, 256), F32)
            for c in range(8):
                acc = acc + dot(at_halo[rows, 256 * c : 256 * c + 256], gagg[256 * c : 256 * c + 256, :])
            outg[pl.ds(n * 32, 32)] = to_blocks(acc)
        send_round(steps, outg, retb, s2, q2)

    give_back(ROUNDS[0])
    give_back(ROUNDS[1])

    def weights(c, carry):
        acc_self, acc_neigh, acc_bias = carry
        rows = pl.ds(pl.multiple_of(c * 256, 256), 256)
        gp = gpre[rows, :]
        acc_self = acc_self + dot_rows(feat[pl.ds(2 * c, 2)].reshape(256, 256), gp)
        acc_neigh = acc_neigh + dot_rows(mean[rows, :], gp)
        acc_bias = acc_bias + jnp.sum(gp.astype(F32).reshape(32, 8, 256), axis=0)
        return acc_self, acc_neigh, acc_bias

    zero = jnp.zeros((256, 256), F32)
    acc_self, acc_neigh, acc_bias = lax.fori_loop(0, 8, weights, (zero, zero, jnp.zeros((8, 256), F32)))
    part[0:16] = acc_self.reshape(16, 16, WIDTH)
    part[16:32] = acc_neigh.reshape(16, 16, WIDTH)
    bias_row = jnp.sum(acc_bias, axis=0, keepdims=True)

    spot = g * 4 + y
    b_shares[spot] = jnp.concatenate([bias_row[:, :128], bias_row[:, 128:], jnp.zeros((6, 128), F32)], axis=0)

    def send_share(t, carry):
        o = lax.rem(spot + t, OWNERS)
        pltpu.make_async_remote_copy(
            part.at[o], shares.at[spot], sr.at[0], qr.at[0], device_id=(o // 4) * 32 + z * 4 + o % 4, device_id_type=FLAT
        ).start()
        return carry

    lax.fori_loop(1, OWNERS, send_share, 0)
    shares[spot] = part[spot]

    @pl.when(spot != 0)
    def _():
        pltpu.make_async_remote_copy(
            b_shares.at[spot], b_shares.at[spot], sr.at[3], qr.at[3], device_id=z * 4, device_id_type=FLAT
        ).start()

    give_back(ROUNDS[2])
    give_back(ROUNDS[3])
    give_back(ROUNDS[4])
    own2 = pltpu.make_async_copy(outg.at[me], retb.at[me], lsem.at[5])
    own2.start()

    def batch(n, sem, dst):
        return pltpu.make_async_remote_copy(
            dst.at[pl.ds(0, n)], dst.at[pl.ds(0, n)], sr.at[sem], qr.at[sem], device_id=flat, device_id_type=FLAT
        )

    batch(31, 0, shares).wait_recv()
    acc = shares[0]
    for o in range(1, OWNERS):
        acc = acc + shares[o]
    layers[z] = acc

    def send_layer(t, carry):
        to = lax.rem(z + t, 8)
        pltpu.make_async_remote_copy(
            layers.at[z], layers.at[z], sr.at[1], qr.at[1], device_id=g * 32 + to * 4 + y, device_id_type=FLAT
        ).start()
        return carry

    lax.fori_loop(1, 8, send_layer, 0)

    @pl.when(spot == 0)
    def _():
        batch(31, 3, b_shares).wait_recv()
        total_bias = b_shares[0]
        for o in range(1, OWNERS):
            total_bias = total_bias + b_shares[o]
        b_layers[z] = total_bias

        def send_bias(t, carry):
            to = lax.rem(z + t, 8)
            pltpu.make_async_remote_copy(
                b_layers.at[z], b_layers.at[z], sr.at[4], qr.at[4], device_id=to * 4, device_id_type=FLAT
            ).start()
            return carry

        lax.fori_loop(1, 8, send_bias, 0)

    def settle(steps, last=False):
        planes, spots = [], []
        for dz in steps:
            plane(dz, outg, retb, s2, q2).wait_recv()
            n = (z + 8 - dz) % 8
            planes.append(from_blocks(retb[pl.ds(n * 32, 32)]))
            spots.append(pl.ds(pl.multiple_of(n * 256, 256), 256))
        for c in range(8):
            at = slice(256 * c, 256 * c + 256)
            acc = total[at, :]
            for place, rows in zip(spots, planes):
                acc = acc + dot(oht[at, place], rows)
            if last:
                gf_ref[at, :] = acc.astype(BF16)
            else:
                total[at, :] = acc

    def base(n, carry):
        rows = pl.ds(pl.multiple_of(n * 256, 256), 256)
        acc = dot_cols(gpre[rows, :], ws_ref[...])
        for c in range(8):
            acc = acc + dot(at_own[rows, 256 * c : 256 * c + 256], gagg[256 * c : 256 * c + 256, :])
        total[rows, :] = acc
        return carry

    lax.fori_loop(0, 8, base, 0)

    batch(7, 1, layers).wait_recv()
    acc = layers[0]
    for k in range(1, 8):
        acc = acc + layers[k]
    factor = 1.0 / math.sqrt(ROWS * 256)
    done[spot] = (acc * factor).astype(done.dtype)

    def send_done(t, carry):
        o = lax.rem(spot + t, OWNERS)
        pltpu.make_async_remote_copy(
            done.at[spot], done.at[spot], sr.at[2], qr.at[2], device_id=(o // 4) * 32 + z * 4 + o % 4, device_id_type=FLAT
        ).start()
        return carry

    lax.fori_loop(1, OWNERS, send_done, 0)

    @pl.when(spot == 0)
    def _():
        batch(7, 4, b_layers).wait_recv()
        total_bias = b_layers[0]
        for k in range(1, 8):
            total_bias = total_bias + b_layers[k]
        b_done[0] = total_bias * factor

        def send_bias(o, carry):
            pltpu.make_async_remote_copy(
                b_done.at[0], b_done.at[0], sr.at[5], qr.at[5], device_id=(o // 4) * 32 + z * 4 + o % 4, device_id_type=FLAT
            ).start()
            return carry

        lax.fori_loop(1, OWNERS, send_bias, 0)

    settle(ROUNDS[0])
    settle(ROUNDS[1])
    settle(ROUNDS[2])
    settle(ROUNDS[3])
    own2.wait()
    settle(ROUNDS[4], True)

    batch(31, 2, done).wait_recv()
    gs_ref[...] = done[0:16].astype(F32).reshape(WIDTH, WIDTH)
    gn_ref[...] = done[16:32].astype(F32).reshape(WIDTH, WIDTH)

    @pl.when(spot != 0)
    def _():
        batch(1, 5, b_done).wait_recv()

    gb_ref[:, :128] = b_done[0, 0:1]
    gb_ref[:, 128:] = b_done[0, 1:2]

    for dz in range(8):
        plane(dz, outb, halob, s1, q1).wait_send()
        plane(dz, outg, retb, s2, q2).wait_send()
    batch(31, 0, shares).wait_send()
    batch(7, 1, layers).wait_send()
    batch(31, 2, done).wait_send()

    @pl.when(spot != 0)
    def _():
        batch(1, 3, b_shares).wait_send()

    @pl.when(spot == 0)
    def _():
        batch(7, 4, b_layers).wait_send()
        batch(31, 5, b_shares).wait_send()


def hand_over(*refs):
    sems = refs[10]
    copies = [pltpu.make_async_copy(refs[n], refs[5 + n], sems.at[n]) for n in range(5)]
    for copy in copies:
        copy.start()
    for copy in copies:
        copy.wait()


def local(
    features, w_self, w_neigh, node_bias, grad_out, send_rows, send_count, adjacency, tile_source
):
    vmem, hbm = pl.BlockSpec(memory_space=pltpu.VMEM), pl.BlockSpec(memory_space=pl.ANY)
    tall = (ROWS, WIDTH)
    blocks = (256, 16, 128)
    dma = pltpu.SemaphoreType.DMA
    shapes = [
        jax.ShapeDtypeStruct(tall, BF16),
        jax.ShapeDtypeStruct(tall, BF16),
        jax.ShapeDtypeStruct((WIDTH, WIDTH), F32),
        jax.ShapeDtypeStruct((WIDTH, WIDTH), F32),
        jax.ShapeDtypeStruct((1, WIDTH), F32),
    ]
    made = pl.pallas_call(
        kernel,
        out_shape=[pltpu.VMEM(a.shape, a.dtype) for a in shapes],
        in_specs=[vmem, vmem, pl.BlockSpec(memory_space=pltpu.SMEM), vmem, vmem, vmem, hbm, hbm, hbm],
        out_specs=[vmem] * 5,
        scratch_shapes=[
            pltpu.VMEM((TILES, EDGE, WIDTH), BF16),
            pltpu.VMEM(tall, BF16),
            pltpu.VMEM((TILES, 2, EDGE, EDGE), jnp.int32),
            pltpu.VMEM((32, 64, 128), jnp.int16),
            pltpu.VMEM(blocks, BF16),
            pltpu.VMEM(blocks, BF16),
            pltpu.VMEM(blocks, BF16),
            pltpu.VMEM(blocks, BF16),
            pltpu.VMEM((TILES, EDGE, WIDTH), BF16),
            pltpu.VMEM((TILES, EDGE, EDGE), BF16),
            pltpu.VMEM((ROWS, ROWS), BF16),
            pltpu.VMEM((ROWS, ROWS), BF16),
            pltpu.VMEM((ROWS, EDGE), F32),
            pltpu.VMEM(tall, F32),
            pltpu.VMEM(tall, F32),
            pltpu.VMEM(tall, BF16),
            pltpu.VMEM(tall, BF16),
            pltpu.VMEM(tall, BF16),
            pltpu.VMEM(tall, F32),
            pltpu.VMEM((ROWS, ROWS), BF16),
            pltpu.VMEM((16, 128), jnp.int32),
            pltpu.VMEM((OWNERS, 16, WIDTH), F32),
            pltpu.VMEM((OWNERS, 16, WIDTH), F32),
            pltpu.VMEM((8, 16, WIDTH), F32),
            pltpu.VMEM((OWNERS, 16, WIDTH), BF16),
            pltpu.VMEM((OWNERS, 8, 128), F32),
            pltpu.VMEM((8, 8, 128), F32),
            pltpu.VMEM((1, 8, 128), F32),
            dma((7,)),
            dma((8,)),
            dma((8,)),
            dma((8,)),
            dma((8,)),
            dma((6,)),
            dma((6,)),
        ],
        compiler_params=pltpu.CompilerParams(
            collective_id=0, has_side_effects=True, vmem_limit_bytes=54 << 20
        ),
        name="sage_layer",
    )(
        send_rows[0].transpose(1, 2, 0), send_count[0].T, tile_source[0].T, node_bias.reshape(1, WIDTH), w_self, w_neigh, features.reshape(TILES, EDGE, WIDTH), grad_out, adjacency[0]
    )
    out, gf, gs, gn, gb = pl.pallas_call(
        hand_over,
        out_shape=shapes,
        in_specs=[vmem] * 5,
        out_specs=[hbm] * 5,
        scratch_shapes=[dma((5,))],
        compiler_params=pltpu.CompilerParams(vmem_limit_bytes=4 << 20),
        name="hand_over",
    )(*made)
    return out, gf, gs, gn, gb.reshape(WIDTH)


def solution(mesh):
    rows = P(("group", "inner"), None)
    placed = (
        rows,
        P(),
        P(),
        P(),
        rows,
        P(("group", "inner"), None, None, None),
        P(("group", "inner"), None, None),
        P(("group", "inner"), None, None, None, None),
        P(("group", "inner"), None, None),
    )
    return jax.shard_map(
        local, mesh=mesh, in_specs=placed, out_specs=(rows, rows, P(), P(), P()), check_vma=False
    )
```

time: 95.5 us -> 84.4 us (0.88)
  Pallas kernels: 94.8 us -> 83.6 us
    pallas_call x2, Pallas kernels: 94.8 us -> 83.6 us  [the longest x1 82.1 us: local(): pl.pallas_call(kernel, out_shape=[pltpu.VMEM(a.shape, a.dtype) for a in s...]
where the time goes in v4:
time: 84.4 us; the launch traced here: 84.3 us
  Pallas kernels  83.6 us (99%)
    pallas_call x1, Pallas kernels, local(): pl.pallas_call(kernel, out_shape=[pltpu.VMEM(a.shape, a.dtype) for a in s...  82.1 us

profile of v4, /device:TPU:1, one launch (start us, length us, event | category | flops | bytes accessed | tf_op | source)
XLA Modules:
  0.0 84.3 jit_solution(9219279246450508839)
XLA Ops:
  0.6 82.1 %sage_layer.1 = (bf16[2048,256]{1,0:T(8,128)(2,1)S(1)}, bf16[2048,256]{1,0:T(8,128)(2,1)S(1)}, f32[256,256]{1,0:T(8,128)S(1)}, f32[256,256]{1,0:T(8,128)S(1)}, f32[1,256]{1,0:T(1,128)S(1)}) custom-call(s32[8,8,32]{2,1,0:T(8,128)} %bitcast.15, s32[8,32]{1,0:T(8,128)} %bitcast.16, s32[2,16]{1,0:T(2,128)} %bitcast.17, f32[1,256]{1,0:T(1,128)} %bitcast.18, ...), custom_call_target="tpu_custom_call" | custom-call | tf_op jit(solution)/shard_map/sage_layer/pallas_call | solution.py:394
  82.7 1.5 %hand_over.1 = (bf16[2048,256]{1,0:T(8,128)(2,1)}, bf16[2048,256]{1,0:T(8,128)(2,1)}, f32[256,256]{1,0:T(8,128)}, f32[256,256]{1,0:T(8,128)}, f32[1,256]{1,0:T(1,128)}) custom-call(bf16[2048,256]{1,0:T(8,128)(2,1)S(1)} %get-tuple-element.15.refs_0_, bf16[2048,256]{1,0:T(8,128)(2,1)S(1)} %get-tuple-element.16.refs_1_, ...), custom_call_target="tpu_custom_call" | custom-call | tf_op jit(solution)/shard_map/hand_over/pallas_call | solution.py:443

commit v5 on v4

--- a/solution.py
+++ b/solution.py
@@ -11,6 +11,7 @@
 BF16, F32 = jnp.bfloat16, jnp.float32
 ROWS, WIDTH, EDGE, TILES = 2048, 256, 128, 16
 OWNERS = 32
+EARLY = 2
 ROUNDS = ((4,), (3, 5), (2, 6), (1, 7), (0,))
 
 
@@ -155,8 +156,9 @@
     lax.fori_loop(0, 8, spread, 0)
     load_gout.wait()
 
-    own1.wait()
-    for steps in ROUNDS:
+    halo[...] = jnp.zeros_like(halo)
+
+    def take(steps):
         for dz in steps:
             plane(dz, outb, halob, s1, q1).wait_recv()
             n = (z + 8 - dz) % 8
@@ -182,8 +184,6 @@
         gagg[rows, :] = (dot_cols(gp, wn_ref[...]) * scale).astype(BF16)
         return carry
 
-    lax.fori_loop(0, 8, layer, 0, unroll=4)
-
     def give_back(steps):
         for dz in steps:
             n = (z + dz) % 8
@@ -194,8 +194,15 @@
             outg[pl.ds(n * 32, 32)] = to_blocks(acc)
         send_round(steps, outg, retb, s2, q2)
 
-    give_back(ROUNDS[0])
-    give_back(ROUNDS[1])
+    for steps in ROUNDS[:EARLY]:
+        take(steps)
+    lax.fori_loop(0, 8, layer, 0, unroll=4)
+    for steps in ROUNDS[:EARLY]:
+        give_back(steps)
+    own1.wait()
+    for steps in ROUNDS[EARLY:]:
+        take(steps)
+    lax.fori_loop(0, 8, layer, 0, unroll=4)
 
     def weights(c, carry):
         acc_self, acc_neigh, acc_bias = carry
@@ -231,9 +238,8 @@
             b_shares.at[spot], b_shares.at[spot], sr.at[3], qr.at[3], device_id=z * 4, device_id_type=FLAT
         ).start()
 
-    give_back(ROUNDS[2])
-    give_back(ROUNDS[3])
-    give_back(ROUNDS[4])
+    for steps in ROUNDS[EARLY:]:
+        give_back(steps)
     own2 = pltpu.make_async_copy(outg.at[me], retb.at[me], lsem.at[5])
     own2.start()
 

time: 84.4 us -> 84.4 us (level)
  no operation moved by 1% of the time
where the time goes in v5:
time: 84.4 us; the launch traced here: 84.3 us
  Pallas kernels  83.7 us (99%)
    pallas_call x1, Pallas kernels, local(): pl.pallas_call(kernel, out_shape=[pltpu.VMEM(a.shape, a.dtype) for a in s...  82.1 us

profile of v5, /device:TPU:1, one launch (start us, length us, event | category | flops | bytes accessed | tf_op | source)
XLA Modules:
  0.0 84.3 jit_solution(1345609419604203091)
XLA Ops:
  0.6 82.1 %sage_layer.1 = (bf16[2048,256]{1,0:T(8,128)(2,1)S(1)}, bf16[2048,256]{1,0:T(8,128)(2,1)S(1)}, f32[256,256]{1,0:T(8,128)S(1)}, f32[256,256]{1,0:T(8,128)S(1)}, f32[1,256]{1,0:T(1,128)S(1)}) custom-call(s32[8,8,32]{2,1,0:T(8,128)} %bitcast.15, s32[8,32]{1,0:T(8,128)} %bitcast.16, s32[2,16]{1,0:T(2,128)} %bitcast.17, f32[1,256]{1,0:T(1,128)} %bitcast.18, ...), custom_call_target="tpu_custom_call" | custom-call | tf_op jit(solution)/shard_map/sage_layer/pallas_call | solution.py:400
  82.8 1.5 %hand_over.1 = (bf16[2048,256]{1,0:T(8,128)(2,1)}, bf16[2048,256]{1,0:T(8,128)(2,1)}, f32[256,256]{1,0:T(8,128)}, f32[256,256]{1,0:T(8,128)}, f32[1,256]{1,0:T(1,128)}) custom-call(bf16[2048,256]{1,0:T(8,128)(2,1)S(1)} %get-tuple-element.15.refs_0_, bf16[2048,256]{1,0:T(8,128)(2,1)S(1)} %get-tuple-element.16.refs_1_, ...), custom_call_target="tpu_custom_call" | custom-call | tf_op jit(solution)/shard_map/hand_over/pallas_call | solution.py:449

commit v6 on v4

--- a/solution.py
+++ b/solution.py
@@ -11,7 +11,11 @@
 BF16, F32 = jnp.bfloat16, jnp.float32
 ROWS, WIDTH, EDGE, TILES = 2048, 256, 128, 16
 OWNERS = 32
-ROUNDS = ((4,), (3, 5), (2, 6), (1, 7), (0,))
+EARLY = 3
+
+
+def step(u):
+    return 4 + ((u + 1) // 2) * (1 - 2 * (u % 2))
 
 
 def dot(left, right):
@@ -75,8 +79,8 @@
         lanes[n : n + 1, :] = jnp.concatenate([turned[2 * n : 2 * n + 1], turned[2 * n + 1 : 2 * n + 2]], axis=1)
     load_feat.wait()
 
-    def pick(dz):
-        n = (z + dz) % 8
+    def pick(u):
+        n = (z + step(u)) % 8
         slab = col[pl.ds(4 * n, 4)].reshape(256, 128)
         lane = lax.broadcasted_iota(jnp.int32, (256, 128), 1)
         acc = jnp.zeros((256, 256), F32)
@@ -86,35 +90,33 @@
             acc = acc + dot(hot, feat[2 * c : 2 * c + 2].reshape(256, 256))
         outb[pl.ds(n * 32, 32)] = to_blocks(acc)
 
-    pick(ROUNDS[0][0])
+    pick(0)
     pl.semaphore_wait(barrier, 255)
 
-    def send_round(steps, src, dst, ssem, rsem):
+    def send_plane(u, src, dst, ssem, rsem):
         def send(m, carry):
             h = ((cx + m // 8) % 4) * 2 + (cc + m // 4) % 2
-            for dz in steps:
-                i = ((z + dz) % 8) * 4 + (y + m) % 4
-                pltpu.make_async_remote_copy(
-                    src.at[i * 8 + h], dst.at[me], ssem.at[dz], rsem.at[dz], device_id=h * 32 + i, device_id_type=FLAT
-                ).start()
+            i = ((z + step(u)) % 8) * 4 + (y + m) % 4
+            pltpu.make_async_remote_copy(
+                src.at[i * 8 + h], dst.at[me], ssem.at[u], rsem.at[u], device_id=h * 32 + i, device_id_type=FLAT
+            ).start()
             return carry
 
-        if steps[0] == 0:
-            lax.fori_loop(1, 32, send, 0)
-        else:
-            lax.fori_loop(0, 32, send, 0, unroll=2)
-
-    def plane(dz, src, dst, ssem, rsem):
-        n = 32 if dz else 31
+        lax.fori_loop(u // 7, 32, send, 0)
+
+    def plane(u, src, dst, ssem, rsem, n=32):
         return pltpu.make_async_remote_copy(
-            src.at[pl.ds(0, n)], dst.at[pl.ds(0, n)], ssem.at[dz], rsem.at[dz], device_id=flat, device_id_type=FLAT
+            src.at[pl.ds(0, n)], dst.at[pl.ds(0, n)], ssem.at[u], rsem.at[u], device_id=flat, device_id_type=FLAT
         )
 
-    for steps in ROUNDS:
-        for dz in steps:
-            if dz != ROUNDS[0][0]:
-                pick(dz)
-        send_round(steps, outb, halob, s1, q1)
+    send_plane(0, outb, halob, s1, q1)
+
+    def send_rows(u, carry):
+        pick(u)
+        send_plane(u, outb, halob, s1, q1)
+        return carry
+
+    lax.fori_loop(1, 8, send_rows, 0)
     own1 = pltpu.make_async_copy(outb.at[me], halob.at[me], lsem.at[3])
     own1.start()
 
@@ -155,12 +157,16 @@
     lax.fori_loop(0, 8, spread, 0)
     load_gout.wait()
 
-    own1.wait()
-    for steps in ROUNDS:
-        for dz in steps:
-            plane(dz, outb, halob, s1, q1).wait_recv()
-            n = (z + 8 - dz) % 8
-            halo[pl.ds(2 * n, 2)] = from_blocks(halob[pl.ds(n * 32, 32)]).reshape(2, EDGE, WIDTH)
+    halo[...] = jnp.zeros_like(halo)
+
+    def place(u):
+        n = (z + 8 - step(u)) % 8
+        halo[pl.ds(2 * n, 2)] = from_blocks(halob[pl.ds(n * 32, 32)]).reshape(2, EDGE, WIDTH)
+
+    def take(u, carry):
+        plane(u, outb, halob, s1, q1).wait_recv()
+        place(u)
+        return carry
 
     def layer(b, carry):
         rows = pl.ds(pl.multiple_of(b * 256, 256), 256)
@@ -182,20 +188,24 @@
         gagg[rows, :] = (dot_cols(gp, wn_ref[...]) * scale).astype(BF16)
         return carry
 
-    lax.fori_loop(0, 8, layer, 0, unroll=4)
-
-    def give_back(steps):
-        for dz in steps:
-            n = (z + dz) % 8
-            rows = pl.ds(pl.multiple_of(n * 256, 256), 256)
-            acc = jnp.zeros((256, 256), F32)
-            for c in range(8):
-                acc = acc + dot(at_halo[rows, 256 * c : 256 * c + 256], gagg[256 * c : 256 * c + 256, :])
-            outg[pl.ds(n * 32, 32)] = to_blocks(acc)
-        send_round(steps, outg, retb, s2, q2)
-
-    give_back(ROUNDS[0])
-    give_back(ROUNDS[1])
+    def give_back(u, carry):
+        n = (z + step(u)) % 8
+        rows = pl.ds(pl.multiple_of(n * 256, 256), 256)
+        acc = jnp.zeros((256, 256), F32)
+        for c in range(8):
+            acc = acc + dot(at_halo[rows, 256 * c : 256 * c + 256], gagg[256 * c : 256 * c + 256, :])
+        outg[pl.ds(n * 32, 32)] = to_blocks(acc)
+        send_plane(u, outg, retb, s2, q2)
+        return carry
+
+    lax.fori_loop(0, EARLY, take, 0)
+    lax.fori_loop(0, 8, layer, 0, unroll=2)
+    lax.fori_loop(0, EARLY, give_back, 0)
+    lax.fori_loop(EARLY, 7, take, 0)
+    own1.wait()
+    plane(7, outb, halob, s1, q1, 31).wait_recv()
+    place(7)
+    lax.fori_loop(0, 8, layer, 0, unroll=2)
 
     def weights(c, carry):
         acc_self, acc_neigh, acc_bias = carry
@@ -231,9 +241,7 @@
             b_shares.at[spot], b_shares.at[spot], sr.at[3], qr.at[3], device_id=z * 4, device_id_type=FLAT
         ).start()
 
-    give_back(ROUNDS[2])
-    give_back(ROUNDS[3])
-    give_back(ROUNDS[4])
+    lax.fori_loop(EARLY, 8, give_back, 0)
     own2 = pltpu.make_async_copy(outg.at[me], retb.at[me], lsem.at[5])
     own2.start()
 
@@ -274,22 +282,22 @@
 
         lax.fori_loop(1, 8, send_bias, 0)
 
-    def settle(steps, last=False):
-        planes, spots = [], []
-        for dz in steps:
-            plane(dz, outg, retb, s2, q2).wait_recv()
-            n = (z + 8 - dz) % 8
-            planes.append(from_blocks(retb[pl.ds(n * 32, 32)]))
-            spots.append(pl.ds(pl.multiple_of(n * 256, 256), 256))
+    def settle(u, last=False):
+        plane(u, outg, retb, s2, q2, 31 if last else 32).wait_recv()
+        n = (z + 8 - step(u)) % 8
+        rows = from_blocks(retb[pl.ds(n * 32, 32)])
+        spots = pl.ds(pl.multiple_of(n * 256, 256), 256)
         for c in range(8):
             at = slice(256 * c, 256 * c + 256)
-            acc = total[at, :]
-            for place, rows in zip(spots, planes):
-                acc = acc + dot(oht[at, place], rows)
+            acc = total[at, :] + dot(oht[at, spots], rows)
             if last:
                 gf_ref[at, :] = acc.astype(BF16)
             else:
                 total[at, :] = acc
+
+    def settle_one(u, carry):
+        settle(u)
+        return carry
 
     def base(n, carry):
         rows = pl.ds(pl.multiple_of(n * 256, 256), 256)
@@ -333,12 +341,9 @@
 
         lax.fori_loop(1, OWNERS, send_bias, 0)
 
-    settle(ROUNDS[0])
-    settle(ROUNDS[1])
-    settle(ROUNDS[2])
-    settle(ROUNDS[3])
+    lax.fori_loop(0, 7, settle_one, 0)
     own2.wait()
-    settle(ROUNDS[4], True)
+    settle(7, True)
 
     batch(31, 2, done).wait_recv()
     gs_ref[...] = done[0:16].astype(F32).reshape(WIDTH, WIDTH)
@@ -351,9 +356,9 @@
     gb_ref[:, :128] = b_done[0, 0:1]
     gb_ref[:, 128:] = b_done[0, 1:2]
 
-    for dz in range(8):
-        plane(dz, outb, halob, s1, q1).wait_send()
-        plane(dz, outg, retb, s2, q2).wait_send()
+    for u in range(8):
+        plane(u, outb, halob, s1, q1, 31 if u == 7 else 32).wait_send()
+        plane(u, outg, retb, s2, q2, 31 if u == 7 else 32).wait_send()
     batch(31, 0, shares).wait_send()
     batch(7, 1, layers).wait_send()
     batch(31, 2, done).wait_send()

time: 84.4 us -> 85.1 us (level)
  no operation moved by 1% of the time
where the time goes in v6:
time: 85.1 us; the launch traced here: 85 us
  Pallas kernels  84.4 us (99%)
    pallas_call x1, Pallas kernels, local(): pl.pallas_call(kernel, out_shape=[pltpu.VMEM(a.shape, a.dtype) for a in s...  82.9 us

profile of v6, /device:TPU:1, one launch (start us, length us, event | category | flops | bytes accessed | tf_op | source)
XLA Modules:
  0.0 85.0 jit_solution(4181569747324525413)
XLA Ops:
  0.6 82.9 %sage_layer.1 = (bf16[2048,256]{1,0:T(8,128)(2,1)S(1)}, bf16[2048,256]{1,0:T(8,128)(2,1)S(1)}, f32[256,256]{1,0:T(8,128)S(1)}, f32[256,256]{1,0:T(8,128)S(1)}, f32[1,256]{1,0:T(1,128)S(1)}) custom-call(s32[8,8,32]{2,1,0:T(8,128)} %bitcast.15, s32[8,32]{1,0:T(8,128)} %bitcast.16, s32[2,16]{1,0:T(2,128)} %bitcast.17, f32[1,256]{1,0:T(1,128)} %bitcast.18, ...), custom_call_target="tpu_custom_call" | custom-call | tf_op jit(solution)/shard_map/sage_layer/pallas_call | solution.py:399
  83.5 1.5 %hand_over.1 = (bf16[2048,256]{1,0:T(8,128)(2,1)}, bf16[2048,256]{1,0:T(8,128)(2,1)}, f32[256,256]{1,0:T(8,128)}, f32[256,256]{1,0:T(8,128)}, f32[1,256]{1,0:T(1,128)}) custom-call(bf16[2048,256]{1,0:T(8,128)(2,1)S(1)} %get-tuple-element.15.refs_0_, bf16[2048,256]{1,0:T(8,128)(2,1)S(1)} %get-tuple-element.16.refs_1_, ...), custom_call_target="tpu_custom_call" | custom-call | tf_op jit(solution)/shard_map/hand_over/pallas_call | solution.py:448
